TPU v7x, 32 devices: a whole 2x2x4 slice. The times are simulated.
32 devices in a mesh: dp: 16 (over z, y, x), seq: 2 (over core).
Axes of the slice: x: 2, y: 2, z: 4, core: 2. Of those that a mesh axis runs over, the one named last changes fastest.
Arguments:
- tokens_in: bfloat16 [8192, 1536], P(('dp', 'seq')), may hold values from -6 to 6
- cotangent: bfloat16 [8192, 1536], P(('dp', 'seq')), may hold values from -6 to 6
- seq_lens: int32 [16, 4], P('dp'), may hold values from 0 to 512, as said below
- in_weight: float32 [1536, 6448], P(('dp', 'seq')), may hold values from -0.15625 to 0.15625
- in_first: float32 [1536, 6448], P(('dp', 'seq')), may hold values from -32 to 32
- in_second: float32 [1536, 6448], P(('dp', 'seq')), may hold values from 54.0672 to 860.16
- out_weight: float32 [3072, 1536], P(('dp', 'seq')), may hold values from -0.109375 to 0.109375
- out_first: float32 [3072, 1536], P(('dp', 'seq')), may hold values from -56 to 56
- out_second: float32 [3072, 1536], P(('dp', 'seq')), may hold values from 172.032 to 2785.28
- conv_weight: float32 [5, 3328], P(None, ('dp', 'seq')), may hold values from -3 to 3
- conv_first: float32 [5, 3328], P(None, ('dp', 'seq')), may hold values from -32 to 32
- conv_second: float32 [5, 3328], P(None, ('dp', 'seq')), may hold values from 77.824 to 1228.8
- gains: float32 [4608], P(('dp', 'seq')), may hold values from 0.25 to 1.75
- gain_first: float32 [4608], P(('dp', 'seq')), may hold values from -48 to 48
- gain_second: float32 [4608], P(('dp', 'seq')), may hold values from 139.264 to 2211.84
- head_params: float32 [3, 48], replicated, may hold values from -8 to 2.5, as said below
- head_first: float32 [3, 48], replicated, may hold values from -96.302287 to 96.302287, as said below
- head_second: float32 [3, 48], replicated, may hold values from 54.272 to 108926.075, as said below
Outputs:
- mixed_out: bfloat16 [8192, 1536], P(('dp', 'seq'))
- grad_input: float32 [8192, 1536], P(('dp', 'seq'))
- in_weight_new: float32 [1536, 6448], P(('dp', 'seq'))
- in_first_new: float32 [1536, 6448], P(('dp', 'seq'))
- in_second_new: float32 [1536, 6448], P(('dp', 'seq'))
- out_weight_new: float32 [3072, 1536], P(('dp', 'seq'))
- out_first_new: float32 [3072, 1536], P(('dp', 'seq'))
- out_second_new: float32 [3072, 1536], P(('dp', 'seq'))
- conv_weight_new: float32 [5, 3328], P(None, ('dp', 'seq'))
- conv_first_new: float32 [5, 3328], P(None, ('dp', 'seq'))
- conv_second_new: float32 [5, 3328], P(None, ('dp', 'seq'))
- gains_new: float32 [4608], P(('dp', 'seq'))
- gain_first_new: float32 [4608], P(('dp', 'seq'))
- gain_second_new: float32 [4608], P(('dp', 'seq'))
- head_params_new: float32 [3, 48], replicated
- head_first_new: float32 [3, 48], replicated
- head_second_new: float32 [3, 48], replicated
Inputs may be any that keep to these rules, and one draw needn't show every extreme that they name: `seq_lens`: row g lists group g's sequences in order, 0 marking an unused slot. Each takes ceil(length / 256) whole blocks of 256 positions after the earlier ones, all within 512 positions; the first is longer than 256; in some group it fills all 512. `head_params`: row 0 shifts the step sizes, row 1 is the logarithm of the decay rates, row 2 holds positive skip gains. `head_first`: both signs. `head_second`: Positive.
All inputs are finite; a program needn't handle non-finite values.
Results may differ from a plain program's by a relative error of at most 0.012.
Values may be sent and summed in bfloat16 or wider, within the bound.
A program may use at most 256 MiB of HBM per device.

v0:
```python
import jax
import jax.numpy as jnp
from jax import lax
from jax.sharding import PartitionSpec as P

D = 1536
HEADS = 48
HDIM = 64
NST = 128
KCONV = 4
BLOCK = 256
SLOTS = 4
STEP = 10
DIN = 3072
CONVC = 3328


highest = lax.Precision.HIGHEST
norm_eps = 1e-05
beta_first = 0.9
beta_second = 0.95
adam_eps = 1e-08
weight_decay = 0.1
rate_in = 0.01
rate_out = 0.008
rate_conv = 0.2
rate_gain = 0.4
rate_head = 0.5


def from_behind(block, axis, distance):
    devices = range(lax.axis_size(axis))
    route = [(i - distance, i) for i in devices if i - distance in devices]
    return lax.ppermute(block, axis, route)


def prefix(value, axis, join, neutral):
    place = lax.axis_index(axis)
    gathered = jax.tree.map(
        lambda a, kind: lax.all_gather(a.astype(kind), axis),
        value,
        jax.tree.map(lambda a: jnp.bfloat16 if a.dtype == jnp.float32 else a.dtype, value),
    )
    state = jax.tree.map(lambda a, e: jnp.zeros_like(a) + jnp.asarray(e, a.dtype), value, neutral)

    def one(hop, state):
        return join(
            state,
            jax.tree.map(
                lambda a, own: lax.dynamic_index_in_dim(a, hop, 0, False).astype(own.dtype),
                gathered,
                value,
            ),
        )

    return lax.fori_loop(0, place, one, state)


def prefix_2(value, axis, combine, identity):
    devices, index = (lax.axis_size(axis), lax.axis_index(axis))
    everything = jax.tree.map(
        lambda part, kind: lax.all_gather(part.astype(kind), axis),
        value,
        (jnp.bfloat16, jnp.bfloat16),
    )
    start = jax.tree.map(
        lambda part, zero: jnp.broadcast_to(jnp.asarray(zero, part.dtype), part.shape),
        value,
        identity,
    )

    def hop(k, before):
        at = devices - 1 - k
        reached = at > index
        new = combine(
            before, jax.tree.map(lambda part, own: part[at].astype(own.dtype), everything, value)
        )
        return jax.tree.map(lambda a, b: jnp.where(reached, a, b), new, before)

    return lax.fori_loop(0, devices, hop, start)


def segment_of(seq_row, position):
    blocks = (seq_row + BLOCK - 1) // BLOCK
    ends = jnp.cumsum(blocks) * BLOCK
    starts = ends - blocks * BLOCK
    above = position[:, None] >= starts[None, :]
    inside = above & (position[:, None] < ends[None, :])
    numbers = jnp.arange(1, SLOTS + 1, dtype=jnp.int32)
    labels_of = jnp.sum(jnp.where(inside, numbers[None, :], 0), axis=1)
    live_rows = jnp.sum(
        (above & (position[:, None] < (starts + seq_row)[None, :])).astype(jnp.float32), axis=1
    )
    return (labels_of, live_rows)


def layout(seq_row, position):
    labels_of, live_rows = segment_of(seq_row, position)
    columns = []
    for conv_lag in range(KCONV):
        earlier, unused_live = segment_of(seq_row, position - conv_lag)
        columns.append(((earlier == labels_of) & (labels_of > 0)).astype(jnp.float32))
    return (live_rows, jnp.stack(columns, axis=1))


def pre_norm(token_rows, gain_row):
    scaling = lax.rsqrt(jnp.mean(token_rows * token_rows, axis=1, keepdims=True) + norm_eps)
    return token_rows * scaling * gain_row[None, :]


def gate_norm(mixed, gate_part, gain_row):
    gated = mixed * jax.nn.silu(gate_part)
    scaling = lax.rsqrt(jnp.mean(gated * gated, axis=1, keepdims=True) + norm_eps)
    return gated * scaling * gain_row[None, :]


def mixer_in(extended, step_raw, conv_par, head_values, factors, live_rows):
    row_count = step_raw.shape[0]
    preact = jnp.zeros((row_count, conv_par.shape[1]), jnp.float32) + conv_par[KCONV][None, :]
    for conv_tap in range(KCONV):
        window = lax.slice_in_dim(extended, conv_tap, conv_tap + row_count, axis=0)
        preact = (
            preact
            + conv_par[conv_tap][None, :] * window * factors[:, KCONV - 1 - conv_tap][:, None]
        )
    conv_act = jax.nn.silu(preact)
    step_size = jax.nn.softplus(step_raw + head_values[0][None, :]) * live_rows[:, None]
    logdec = -jnp.exp(head_values[1])[None, :] * step_size
    return (conv_act, step_size, logdec)


def lower_ones():
    row_ids = lax.broadcasted_iota(jnp.int32, (BLOCK, BLOCK), 0)
    col_ids = lax.broadcasted_iota(jnp.int32, (BLOCK, BLOCK), 1)
    return (row_ids >= col_ids).astype(jnp.float32)


def block_state(values, keys_in, step_size, logdec):
    cumul = jnp.dot(lower_ones(), logdec, precision=highest)
    totals = cumul[-1]
    weighting = jnp.exp(totals[None, :] - cumul) * step_size
    states = jnp.einsum("uhp,un->hpn", weighting[:, :, None] * values, keys_in, precision=highest)
    return (jnp.exp(totals), states)


def block_out(values, keys_in, queries, step_size, logdec, skip_gain, start_state):
    lower_tri = lower_ones()
    cumul = jnp.dot(lower_tri, logdec, precision=highest)
    across = cumul.T
    gap_matrix = across[:, :, None] - across[:, None, :]
    decays = jnp.exp(jnp.where(lower_tri[None, :, :] > 0, gap_matrix, -1e30))
    gram_matrix = jnp.dot(queries, keys_in.T, precision=highest)
    mixing = gram_matrix[None, :, :] * decays * step_size.T[:, None, :]
    intra_part = jnp.einsum("htu,uhp->thp", mixing, values, precision=highest)
    carried = jnp.exp(cumul)[:, :, None] * jnp.einsum(
        "tn,hpn->thp", queries, start_state, precision=highest
    )
    return intra_part + carried + skip_gain[None, :, None] * values


def block_full(values, keys_in, queries, step_size, logdec, skip_gain, start_state):
    factor_end, states = block_state(values, keys_in, step_size, logdec)
    outputs = block_out(values, keys_in, queries, step_size, logdec, skip_gain, start_state)
    return (outputs, factor_end[:, None, None] * start_state + states)


def adam_update(weight, first, second, gradient, step_rate):
    first_new = beta_first * first + (1.0 - beta_first) * gradient
    second_new = beta_second * second + (1.0 - beta_second) * gradient * gradient
    first_hat = first_new / (1.0 - beta_first**STEP)
    second_hat = second_new / (1.0 - beta_second**STEP)
    weight_new = weight - step_rate * (
        first_hat / (jnp.sqrt(second_hat) + adam_eps) + weight_decay * weight
    )
    return (weight_new, first_new, second_new)


def carry_join(earlier, later):
    return (earlier[0] * later[0], later[0][:, None, None] * earlier[1] + later[1])


def as_float(array_low):
    return lax.optimization_barrier(array_low).astype(jnp.float32)


def contract_rows(left, right):
    return lax.dot_general(
        left, right, (((0,), (0,)), ((), ())), preferred_element_type=jnp.float32
    )


def contract_cols(left, right):
    return lax.dot_general(
        left, right, (((1,), (1,)), ((), ())), preferred_element_type=jnp.float32
    )


def per_device(
    tokens_in,
    cotangent,
    seq_lens,
    in_weight,
    in_first,
    in_second,
    out_weight,
    out_first,
    out_second,
    conv_weight,
    conv_first,
    conv_second,
    gains,
    gain_first,
    gain_second,
    head_params,
    head_first,
    head_second,
):
    local_tok = tokens_in.shape[0]
    position = lax.axis_index("seq") * local_tok + jnp.arange(local_tok, dtype=jnp.int32)
    live_rows, factors = layout(seq_lens[0], position)
    low_weights = (
        in_weight.astype(jnp.bfloat16),
        out_weight.astype(jnp.bfloat16),
        conv_weight.astype(jnp.bfloat16),
        gains.astype(jnp.bfloat16),
    )
    in_full, out_full, conv_full, gain_full = (
        lax.all_gather(low_weights[0], ("dp", "seq"), axis=0, tiled=True),
        lax.all_gather(low_weights[1], ("dp", "seq"), axis=0, tiled=True),
        lax.all_gather(low_weights[2], ("dp", "seq"), axis=1, tiled=True),
        lax.all_gather(low_weights[3], ("dp", "seq"), axis=0, tiled=True),
    )
    conv_par = conv_full.astype(jnp.float32)
    gain_par = gain_full.astype(jnp.float32)
    token_rows = tokens_in.astype(jnp.float32)
    normed_value, pull_pre = jax.vjp(pre_norm, token_rows, gain_par[:D])
    normed = normed_value.astype(jnp.bfloat16)
    projected = jnp.dot(normed, in_full, preferred_element_type=jnp.float32)
    gate_part = projected[:, :DIN]
    conv_in = projected[:, DIN : DIN + CONVC]
    step_raw = projected[:, DIN + CONVC :]
    halo_rows = from_behind(conv_in[local_tok - KCONV + 1 :], "seq", 1)
    extended = jnp.concatenate([halo_rows, conv_in], axis=0)

    def mixer_local(extended_rows, raw_steps, conv_values, head_values):
        return mixer_in(extended_rows, raw_steps, conv_values, head_values, factors, live_rows)

    (conv_act, step_size, logdec), pull_mixer = jax.vjp(
        mixer_local, extended, step_raw, conv_par, head_params
    )
    conv_used = as_float(conv_act.astype(jnp.bfloat16))
    block_count = local_tok // BLOCK
    values = conv_used[:, :DIN].reshape(block_count, BLOCK, HEADS, HDIM)
    keys_in = conv_used[:, DIN : DIN + NST].reshape(block_count, BLOCK, NST)
    queries = conv_used[:, DIN + NST :].reshape(block_count, BLOCK, NST)
    steps_blk = step_size.reshape(block_count, BLOCK, HEADS)
    logdec_blk = logdec.reshape(block_count, BLOCK, HEADS)
    resets = factors[::BLOCK, 1]
    skip_gain = head_params[2]
    decays, block_states = jax.vmap(block_state)(values, keys_in, steps_blk, logdec_blk)

    def fold_local(carried, block_item):
        factor_now = block_item[0] * block_item[2]
        return (
            (carried[0] * factor_now, factor_now[:, None, None] * carried[1] + block_item[1]),
            None,
        )

    identity = (jnp.ones((HEADS,), jnp.float32), jnp.zeros((HEADS, HDIM, NST), jnp.float32))
    device_sum, unused_fold = lax.scan(fold_local, identity, (decays, block_states, resets))
    unused_dec, entering = prefix(device_sum, "seq", carry_join, identity)

    def start_states(states, block_item):
        begin = block_item[2] * states
        return (block_item[0][:, None, None] * begin + block_item[1], begin)

    unused_end, begins = lax.scan(start_states, entering, (decays, block_states, resets))

    def emit(block_item):
        return block_out(
            block_item[0],
            block_item[1],
            block_item[2],
            block_item[3],
            block_item[4],
            skip_gain,
            block_item[5],
        )

    mixed = lax.map(emit, (values, keys_in, queries, steps_blk, logdec_blk, begins)).reshape(
        local_tok, DIN
    )
    normed_out_value, pull_gate = jax.vjp(gate_norm, mixed, gate_part, gain_par[D:])
    normed_out = normed_out_value.astype(jnp.bfloat16)
    branch = jnp.dot(normed_out, out_full, preferred_element_type=jnp.float32)
    mixed_out = (token_rows + live_rows[:, None] * branch).astype(jnp.bfloat16)
    out_grad = (cotangent.astype(jnp.float32) * live_rows[:, None]).astype(jnp.bfloat16)
    in_back, out_back = (
        lax.all_gather(in_weight.astype(jnp.bfloat16), ("dp", "seq"), axis=0, tiled=True),
        lax.all_gather(out_weight.astype(jnp.bfloat16), ("dp", "seq"), axis=0, tiled=True),
    )
    grad_out_w = contract_rows(normed_out, out_grad)
    grad_normed_out = contract_cols(out_grad, out_back)
    grad_mixed, grad_gate, grad_gain_in = pull_gate(grad_normed_out)
    mixed_back = as_float(grad_mixed.astype(jnp.bfloat16)).reshape(block_count, BLOCK, HEADS, HDIM)

    def adjoint_local(carried, block_item):
        cumul = jnp.dot(lower_ones(), block_item[2], precision=highest)
        weighted = jnp.exp(cumul)[:, :, None] * block_item[0]
        direct = jnp.einsum("thp,tn->hpn", weighted, block_item[1], precision=highest)
        return (block_item[4] * (direct + block_item[3][:, None, None] * carried), None)

    local_adj, unused_adj = lax.scan(
        adjoint_local, identity[1], (mixed_back, queries, logdec_blk, decays, resets), reverse=True
    )
    unused_later, leaving = prefix_2((device_sum[0], local_adj), "seq", carry_join, identity)

    def adjoint_block(carried, block_item):
        unused_primal, pull_block = jax.vjp(
            block_full,
            block_item[0],
            block_item[1],
            block_item[2],
            block_item[3],
            block_item[4],
            skip_gain,
            block_item[5],
        )
        grads = pull_block((block_item[6], carried[0]))
        return ((block_item[7] * grads[6], carried[1] + grads[5]), grads[:5])

    (unused_state, grad_skip), block_grads = lax.scan(
        adjoint_block,
        (leaving, jnp.zeros((HEADS,), jnp.float32)),
        (values, keys_in, queries, steps_blk, logdec_blk, begins, mixed_back, resets),
        reverse=True,
    )
    grad_values, grad_keys, grad_queries, grad_step, grad_logdec = block_grads
    grad_act = jnp.concatenate(
        [
            grad_values.reshape(local_tok, DIN),
            grad_keys.reshape(local_tok, NST),
            grad_queries.reshape(local_tok, NST),
        ],
        axis=1,
    )
    grad_ext, grad_raw, grad_conv, grad_head_part = pull_mixer(
        (grad_act, grad_step.reshape(local_tok, HEADS), grad_logdec.reshape(local_tok, HEADS))
    )
    returned = from_behind(grad_ext[: KCONV - 1].astype(jnp.bfloat16), "seq", -1).astype(
        jnp.float32
    )
    grad_conv_in = grad_ext[KCONV - 1 :] + jnp.concatenate(
        [jnp.zeros((local_tok - KCONV + 1, CONVC), jnp.float32), returned], axis=0
    )
    grad_proj = jnp.concatenate([grad_gate, grad_conv_in, grad_raw], axis=1).astype(jnp.bfloat16)
    grad_normed = contract_cols(grad_proj, in_back)
    grad_rows, grad_gain_pre = pull_pre(grad_normed)
    grad_input = cotangent.astype(jnp.float32) + grad_rows
    grad_gains = jnp.concatenate([grad_gain_pre, grad_gain_in], axis=0)
    grad_head = jnp.concatenate(
        [grad_head_part[:2], (grad_head_part[2] + grad_skip)[None, :]], axis=0
    )
    grad_in_w = contract_rows(normed, grad_proj)
    in_sum, out_sum, conv_sum, gain_sum = (
        lax.psum_scatter(grad_in_w, ("dp", "seq"), scatter_dimension=0, tiled=True),
        lax.psum_scatter(grad_out_w, ("dp", "seq"), scatter_dimension=0, tiled=True),
        lax.psum_scatter(grad_conv, ("dp", "seq"), scatter_dimension=1, tiled=True),
        lax.psum_scatter(grad_gains, ("dp", "seq"), scatter_dimension=0, tiled=True),
    )
    head_sum = lax.psum(grad_head, ("dp", "seq"))
    new_in = adam_update(in_weight, in_first, in_second, in_sum, rate_in)
    new_out = adam_update(out_weight, out_first, out_second, out_sum, rate_out)
    new_conv = adam_update(conv_weight, conv_first, conv_second, conv_sum, rate_conv)
    new_gain = adam_update(gains, gain_first, gain_second, gain_sum, rate_gain)
    new_head = adam_update(head_params, head_first, head_second, head_sum, rate_head)
    return (
        mixed_out,
        grad_input,
        new_in[0],
        new_in[1],
        new_in[2],
        new_out[0],
        new_out[1],
        new_out[2],
        new_conv[0],
        new_conv[1],
        new_conv[2],
        new_gain[0],
        new_gain[1],
        new_gain[2],
        new_head[0],
        new_head[1],
        new_head[2],
    )


def solution(mesh):
    placed = (
        P(("dp", "seq"), None),
        P(("dp", "seq"), None),
        P("dp", None),
        P(("dp", "seq"), None),
        P(("dp", "seq"), None),
        P(("dp", "seq"), None),
        P(("dp", "seq"), None),
        P(("dp", "seq"), None),
        P(("dp", "seq"), None),
        P(None, ("dp", "seq")),
        P(None, ("dp", "seq")),
        P(None, ("dp", "seq")),
        P(("dp", "seq")),
        P(("dp", "seq")),
        P(("dp", "seq")),
        P(),
        P(),
        P(),
    )
    return jax.shard_map(
        per_device,
        mesh=mesh,
        in_specs=placed,
        out_specs=(
            P(("dp", "seq"), None),
            P(("dp", "seq"), None),
            P(("dp", "seq"), None),
            P(("dp", "seq"), None),
            P(("dp", "seq"), None),
            P(("dp", "seq"), None),
            P(("dp", "seq"), None),
            P(("dp", "seq"), None),
            P(None, ("dp", "seq")),
            P(None, ("dp", "seq")),
            P(None, ("dp", "seq")),
            P(("dp", "seq")),
            P(("dp", "seq")),
            P(("dp", "seq")),
            P(),
            P(),
            P(),
        ),
        check_vma=False,
    )
```

profile of v0, /device:TPU:0, one launch (start us, length us, event | category | flops | bytes accessed | tf_op | source)
XLA Modules:
  0.0 1123.9 jit_solution(11452810520708739579)
XLA Ops:
  7.3 2.3 convert_element_type.169
  13.2 43.0 %all-reduce.13 = bf16[4608]{0:T(1024)(128)(2,1)S(1)} all-reduce(bf16[4608]{0:T(1024)(128)(2,1)S(1)} %dynamic-update-slice), channel_id=1, replica_groups=mesh['dp'=16,'seq'=2] {'dp','seq'}, use_global_device_ids=true, to_apply=%add.13 | all-reduce | flops 4608 | bytes 18432
  56.9 40.8 %all-gather.2 = bf16[32,104,5]{1,2,0:T(8,128)(2,1)S(1)} all-gather(bf16[1,104,5]{1,2,0:T(8,128)(2,1)S(1)} %convert_bitcast_fusion), channel_id=1, replica_groups=mesh['dp'=16,'seq'=2] {'dp','seq'}, dimensions={0}, use_global_device_ids=true | all-gather | bytes 34320 | tf_op jit(solution)/shard_map/all_gather | solution.py:230
  99.5 46.6 %all-gather.9.cloned.1.call-done = bf16[1536,6448]{1,0:T(8,128)(2,1)} async-done(((bf16[48,6448]{1,0:T(8,128)(2,1)}), bf16[1536,6448]{1,0:T(8,128)(2,1)}) %all-gather.9.cloned.1.call-update) | async-done | bytes 19808272 | tf_op jit(solution)/shard_map/all_gather | solution.py:228
  146.1 13.0 %fusion.79 = f32[256,6448]{0,1:T(8,128)S(1)} fusion(bf16[1536,6448]{1,0:T(8,128)(2,1)} %all-gather.9.cloned.1.call-done, bf16[256,1536]{1,0:T(8,128)(2,1)} %param.22, f32[1536]{0:T(1024)S(1)} %slice.117, f32[256]{0:T(256)S(1)} %fusion.117), kind=kOutput, calls=%fused_computation.131 | convolution fusion | flops 5072486400 | bytes 27204608 | tf_op jit(solution)/shard_map/dot_general | solution.py:238
  159.2 2.7 copy-done.3
  161.9 1.7 slice.118
  163.6 2.6 copy.79
  166.2 2.8 collective-permute-start
  169.0 1.1 fusion.77
  170.1 1.4 multiply_reduce_fusion.14
  172.0 1.5 fusion.126
  173.5 2.2 slice.119
  175.8 2.6 copy.80
  178.4 10.2 multiply_convert_fusion
  188.9 1.0 copy-done.6
  189.8 2.4 add_convert_fusion
  193.2 2.0 all-gather.3
  195.8 1.8 fusion.102
  197.6 3.4 fusion.137
  201.3 3.6 fusion.56
  205.0 9.5 fusion.30
  214.6 4.1 multiply_reduce_fusion.11
  218.7 1.7 copy-done
  220.4 8.2 fusion.72
  228.7 209.1 %reduce-scatter.6.cloned.1.call-done = f32[96,1536]{1,0:T(8,128)} async-done(((f32[3072,1536]{1,0:T(8,128)}), f32[96,1536]{1,0:T(8,128)}) %reduce-scatter.6.cloned.1.call-update) | async-done | bytes 589840 | tf_op jit(solution)/shard_map/reduce_scatter | solution.py:367
  437.8 2.7 multiply_subtract_fusion.1
  440.5 81.7 %all-gather.11.cloned.1.call-done = bf16[3072,1536]{1,0:T(8,128)(2,1)} async-done(((bf16[96,1536]{1,0:T(8,128)(2,1)}), bf16[3072,1536]{1,0:T(8,128)(2,1)}) %all-gather.11.cloned.1.call-update) | async-done | bytes 9437200 | tf_op jit(solution)/shard_map/all_gather | solution.py:229
  522.2 8.8 multiply_reduce_fusion.7
  531.0 4.9 fusion.28
  535.9 1.5 multiply_reduce_fusion.8
  537.4 1.7 copy-done.9
  539.1 4.0 multiply_convert_fusion.3
  543.1 8.5 all-reduce.19.cloned.1.call-start
  551.6 10.6 fusion.8
  562.2 0.8 fusion.76
  563.1 3.6 fusion.64
  566.7 1.8 convolution_add_fusion
  568.5 4.4 while.19
  569.1 1.5 fusion.152
  571.4 1.5 fusion.152
  572.9 1.7 multiply_reduce_fusion.12
  574.8 4.6 multiply_reduce_fusion.9
  579.4 3.6 fusion.61
  583.8 1.0 fusion.136
  585.0 11.3 %fusion.29 = f32[256,48,64]{0,2,1:T(8,128)} fusion(f32[256,48,64]{0,2,1:T(8,128)} %get-tuple-element.445, f32[256,48,64]{0,2,1:T(8,128)} %copy-done.9, bf16[48,64,256]{2,1,0:T(8,128)(2,1)S(1)} %bitcast.141, f32[48,256]{1,0:T(8,128)} %get-tuple-element.426, f32[48,256]{1,0:T(8,128)S(1)} %bitcast.150, f32[256,256]{1,0:T(8,128)} %fusion.102, ...), kind=kOutput, calls=%fused_computation.59 | convolution fusion | flops 2431647744 | bytes 11485376 | tf_op jit(solution)/shard_map/while/body/eval_jaxpr/transpose(jvp(htu,uhp->thp))/dot_general | solution.py:154
  596.3 1.1 convolution_add_fusion.1
  597.5 10.0 multiply_reduce_fusion.4
  607.5 2.4 multiply_multiply_fusion.3
  610.0 4.2 pad_add_fusion
  614.2 2.4 copy-done.11
  617.0 1.3 collective-permute-start.1
  619.3 1.2 fusion.130
  621.0 3.5 fusion.25
  624.5 17.8 %fusion.58 = f32[1536,6448]{1,0:T(8,128)} fusion(bf16[256,48]{0,1:T(8,128)(2,1)S(1)} %get-tuple-element.402, bf16[256,3328]{0,1:T(8,128)(2,1)S(1)} %fusion.25, bf16[256,3072]{0,1:T(8,128)(2,1)} %get-tuple-element.423, bf16[256,1536]{1,0:T(8,128)(2,1)S(1)} %copy-done.18, f32[1536]{0:T(1024)S(1)} %slice.117, f32[256]{0:T(256)S(1)} %copy-done.44), kind=kOutput, calls=%fused_computation.109 | convolution fusion | flops 5082390528 | bytes 43711488 | tf_op jit(solution)/shard_map/dot_general | solution.py:187
  642.4 2.5 multiply_reduce_fusion.6
  645.3 7.5 fusion.38
  652.9 11.8 %fusion.46 = (f32[1536]{0:T(1024)S(1)}, f32[256]{0:T(256)S(1)}, f32[256,1536]{1,0:T(8,128)}) fusion(bf16[256,1536]{1,0:T(8,128)(2,1)} %param.22, f32[256]{0:T(256)S(1)} %copy-done.44, f32[1536]{0:T(1024)S(1)} %slice.117, bf16[1536,6448]{1,0:T(8,128)(2,1)} %all-gather.9.cloned.1.call-done, bf16[256,48]{0,1:T(8,128)(2,1)S(1)} %get-tuple-element.402, ...), kind=kOutput, calls=%fused_computation.96 | convolution fusion | flops 5083568128 | bytes 25483264 | tf_op jit(solution)/shard_map/dot_general | solution.py:193
  664.8 40.1 %all-reduce.16 = (f32[4608]{0:T(1024)S(1)}, f32[3,48]{1,0:T(4,128)S(1)}) all-reduce(f32[4608]{0:T(1024)S(1)} %pad_maximum_fusion.5, f32[3,48]{1,0:T(4,128)S(1)} %pad_maximum_fusion.6), channel_id=7, replica_groups=mesh['dp'=16,'seq'=2] {'dp','seq'}, use_global_device_ids=true, to_apply=%region_32.33.clone | all-reduce | flops 4752 | bytes 38016
  706.2 3.0 convert_add_fusion.3
  709.2 30.2 %all-reduce.19.cloned.1.call-done = f32[5,3328]{1,0:T(8,128)} async-done(((f32[5,3328]{1,0:T(8,128)}), f32[5,3328]{1,0:T(8,128)}) %all-reduce.19.cloned.1.call-update) | async-done | bytes 66576
  739.4 1.4 multiply_subtract_fusion.2
  740.8 371.3 %reduce-scatter.4.cloned.1.call-done = f32[48,6448]{1,0:T(8,128)} async-done(((f32[1536,6448]{1,0:T(8,128)}), f32[48,6448]{1,0:T(8,128)}) %reduce-scatter.4.cloned.1.call-update) | async-done | bytes 1238032 | tf_op jit(solution)/shard_map/reduce_scatter | solution.py:366
  1112.1 4.5 multiply_subtract_fusion
  (224 shorter events, 15.0 us)
Async XLA Ops:
  7.2 91.5 %copy-start.17 = (bf16[256,1536]{1,0:T(8,128)(2,1)S(1)}, bf16[256,1536]{1,0:T(8,128)(2,1)}, u32[]{:S(2)}) copy-start(bf16[256,1536]{1,0:T(8,128)(2,1)} %param.22) | copy-start | bytes 2359300
  7.2 91.7 %copy-start.58 = (f32[3,48]{1,0:T(4,128)S(1)}, f32[3,48]{1,0:T(4,128)}, u32[]{:S(2)}) copy-start(f32[3,48]{1,0:T(4,128)} %param.37) | copy-start | bytes 1732
  7.2 138.9 %all-gather.9.cloned.1.call-start = ((), (), s32[]{:S(2)}) async-start(), calls=%async_computation.2 | async-start | bytes 20680704 | tf_op jit(solution)/shard_map/all_gather | solution.py:228
  9.5 191.5 %all-gather.13.cloned.1.call-start = ((), (), s32[]{:S(2)}) async-start(), calls=%async_computation.6 | async-start | bytes 2359296 | tf_op jit(solution)/shard_map/all_gather | solution.py:40
  11.8 166.6 %copy-start.47 = (f32[256]{0:T(256)}, f32[256]{0:T(256)S(1)}, u32[]{:S(2)}) copy-start(f32[256]{0:T(256)S(1)} %get-tuple-element.439) | copy-start | bytes 3076
  11.8 166.6 %copy-start.49 = (f32[256]{0:T(256)}, f32[256]{0:T(256)S(1)}, u32[]{:S(2)}) copy-start(f32[256]{0:T(256)S(1)} %get-tuple-element.440) | copy-start | bytes 3076
  97.9 73.5 %copy-start.45 = (f32[256]{0:T(256)}, f32[256]{0:T(256)S(1)}, u32[]{:S(2)}) copy-start(f32[256]{0:T(256)S(1)} %convert_reduce_fusion) | copy-start | bytes 3076
  98.9 60.2 %copy-start.56 = (f32[256]{0:T(256)}, f32[256]{0:T(256)S(1)}, u32[]{:S(2)}) copy-start(f32[256]{0:T(256)S(1)} %fusion.48) | copy-start | bytes 3076
  98.9 60.2 %copy-start.43 = (f32[256]{0:T(256)}, f32[256]{0:T(256)S(1)}, u32[]{:S(2)}) copy-start(f32[256]{0:T(256)S(1)} %fusion.117) | copy-start | bytes 3076
  99.5 69.5 %copy-start.60 = (f32[48]{0:T(128)}, f32[48]{0:T(128)S(1)}, u32[]{:S(2)}) copy-start(f32[48]{0:T(128)S(1)} %get-tuple-element.437) | copy-start | bytes 580
  99.5 69.5 %copy-start.73 = (f32[48]{0:T(128)}, f32[48]{0:T(128)S(1)}, u32[]{:S(2)}) copy-start(f32[48]{0:T(128)S(1)} %get-tuple-element.438) | copy-start | bytes 580
  166.2 9.6 collective-permute-start
  175.7 12.9 %copy-start.4 = (f32[256,3328]{0,1:T(8,128)}, f32[256,3328]{0,1:T(8,128)S(1)}, u32[]{:S(2)}) copy-start(f32[256,3328]{0,1:T(8,128)S(1)} %slice.119) | copy-start | bytes 10223620
  192.3 245.5 %reduce-scatter.6.cloned.1.call-start = ((), (), s32[]{:S(2)}) async-start(), calls=%async_computation.5 | async-start | bytes 19464192 | tf_op jit(solution)/shard_map/reduce_scatter | solution.py:367
  192.4 12.5 %copy-start.40 = (pred[256,256]{1,0:T(8,128)(4,1)}, pred[256,256]{1,0:T(8,128)(4,1)S(1)}, u32[]{:S(2)}) copy-start(pred[256,256]{1,0:T(8,128)(4,1)S(1)} %convert_compare_fusion) | copy-start | bytes 196612
  204.9 9.6 copy-start.20
  214.5 5.9 copy-start.24
  214.6 5.9 copy-start.46
  228.6 209.1 %copy-start.27 = (f32[96,1536]{1,0:T(8,128)S(1)}, f32[96,1536]{1,0:T(8,128)}, u32[]{:S(2)}) copy-start(f32[96,1536]{1,0:T(8,128)} %param.28) | copy-start | bytes 1769476
  228.6 209.1 %copy-start.28 = (f32[96,1536]{1,0:T(8,128)S(1)}, f32[96,1536]{1,0:T(8,128)}, u32[]{:S(2)}) copy-start(f32[96,1536]{1,0:T(8,128)} %param.29) | copy-start | bytes 1769476
  228.6 209.1 %copy-start.29 = (f32[96,1536]{1,0:T(8,128)S(1)}, f32[96,1536]{1,0:T(8,128)}, u32[]{:S(2)}) copy-start(f32[96,1536]{1,0:T(8,128)} %param.30) | copy-start | bytes 1769476
  228.6 293.5 %all-gather.11.cloned.1.call-start = ((), (), s32[]{:S(2)}) async-start(), calls=%async_computation.3 | async-start | bytes 9732096 | tf_op jit(solution)/shard_map/all_gather | solution.py:229
  440.4 128.0 %all-gather.15.cloned.1.call-start = ((), (), s32[]{:S(2)}) async-start(), calls=%async_computation.7 | async-start | bytes 2359296 | tf_op jit(solution)/shard_map/all_gather | solution.py:62
  522.2 8.8 copy-start.1
  522.2 8.8 copy-start.16
  531.0 4.9 copy-start.21
  543.1 196.4 %all-reduce.19.cloned.1.call-start = ((), (), s32[]{:S(2)}) async-start(), calls=%async_computation.8 | async-start | bytes 212992
  551.6 10.6 copy-start.36
  551.6 11.4 %copy-start.10 = (f32[256,48,64]{0,2,1:T(8,128)S(1)}, f32[256,48,64]{0,2,1:T(8,128)}, u32[]{:S(2)}) copy-start(f32[256,48,64]{0,2,1:T(8,128)} %copy-done.9) | copy-start | bytes 9437188
  551.6 11.4 %copy-start.33 = (f32[256,48]{0,1:T(8,128)S(1)}, f32[256,48]{0,1:T(8,128)}, u32[]{:S(2)}) copy-start(f32[256,48]{0,1:T(8,128)} %get-tuple-element.435) | copy-start | bytes 147460
  579.4 5.5 copy-start.14
  584.9 11.4 %copy-start.31 = (f32[256,128]{0,1:T(8,128)S(1)}, f32[256,128]{0,1:T(8,128)}, u32[]{:S(2)}) copy-start(f32[256,128]{0,1:T(8,128)} %fusion.61) | copy-start | bytes 393220
  584.9 12.5 %copy-start.5 = (f32[256,3328]{0,1:T(8,128)S(1)}, f32[256,3328]{0,1:T(8,128)}, u32[]{:S(2)}) copy-start(f32[256,3328]{0,1:T(8,128)} %copy-done.4) | copy-start | bytes 10223620
  584.9 12.5 %copy-start.12 = (f32[3,3328]{0,1:T(8,128)S(1)}, f32[3,3328]{0,1:T(8,128)}, u32[]{:S(2)}) copy-start(f32[3,3328]{0,1:T(8,128)} %copy.80) | copy-start | bytes 119812
  584.9 12.5 %copy-start.30 = (f32[256,128]{0,1:T(8,128)S(1)}, f32[256,128]{0,1:T(8,128)}, u32[]{:S(2)}) copy-start(f32[256,128]{0,1:T(8,128)} %convolution_add_fusion) | copy-start | bytes 393220
  584.9 12.5 %copy-start.48 = (f32[256]{0:T(256)S(1)}, f32[256]{0:T(256)}, u32[]{:S(2)}) copy-start(f32[256]{0:T(256)} %copy-done.47) | copy-start | bytes 3076
  584.9 12.5 %copy-start.50 = (f32[256]{0:T(256)S(1)}, f32[256]{0:T(256)}, u32[]{:S(2)}) copy-start(f32[256]{0:T(256)} %copy-done.49) | copy-start | bytes 3076
  585.0 12.5 %copy-start.52 = (f32[256]{0:T(256)S(1)}, f32[256]{0:T(256)}, u32[]{:S(2)}) copy-start(f32[256]{0:T(256)} %get-tuple-element.441) | copy-start | bytes 3076
  585.0 12.5 %copy-start.53 = (f32[256]{0:T(256)S(1)}, f32[256]{0:T(256)}, u32[]{:S(2)}) copy-start(f32[256]{0:T(256)} %get-tuple-element.442) | copy-start | bytes 3076
  597.5 10.0 copy-start.37
  597.5 10.0 copy-start.38
  597.5 10.0 copy-start.39
  609.9 9.4 copy-start.35
  609.9 9.4 copy-start.42
  609.9 9.4 copy-start.63
  609.9 9.4 copy-start.74
  609.9 9.4 copy-start.76
  617.0 3.5 collective-permute-start.1
  619.1 492.9 %reduce-scatter.4.cloned.1.call-start = ((), (), s32[]{:S(2)}) async-start(), calls=%async_computation.4 | async-start | bytes 41361408 | tf_op jit(solution)/shard_map/reduce_scatter | solution.py:366
  624.5 17.9 %copy-start.22 = (bf16[256,3328]{0,1:T(8,128)(2,1)}, bf16[256,3328]{0,1:T(8,128)(2,1)S(1)}, u32[]{:S(2)}) copy-start(bf16[256,3328]{0,1:T(8,128)(2,1)S(1)} %fusion.25) | copy-start | bytes 5111812
  645.3 7.5 copy-start.59
  652.8 12.0 %copy-start.55 = (f32[3072]{0:T(1024)S(1)}, f32[3072]{0:T(1024)}, u32[]{:S(2)}) copy-start(f32[3072]{0:T(1024)} %get-tuple-element.355) | copy-start | bytes 36868
  652.8 52.1 %copy-start.57 = (f32[256]{0:T(256)S(1)}, f32[256]{0:T(256)}, u32[]{:S(2)}) copy-start(f32[256]{0:T(256)} %copy-done.56) | copy-start | bytes 3076
  652.8 52.1 %copy-start.70 = (f32[144]{0:T(256)S(1)}, f32[144]{0:T(256)}, u32[]{:S(2)}) copy-start(f32[144]{0:T(256)} %param.34) | copy-start | bytes 1732
  652.8 52.0 %copy-start.71 = (f32[144]{0:T(256)S(1)}, f32[144]{0:T(256)}, u32[]{:S(2)}) copy-start(f32[144]{0:T(256)} %param.35) | copy-start | bytes 1732
  652.9 52.0 %copy-start.72 = (f32[144]{0:T(256)S(1)}, f32[144]{0:T(256)}, u32[]{:S(2)}) copy-start(f32[144]{0:T(256)} %param.36) | copy-start | bytes 1732
  652.9 52.7 %copy-start.66 = (f32[3,48]{1,0:T(4,128)S(1)}, f32[3,48]{1,0:T(4,128)}, u32[]{:S(2)}) copy-start(f32[3,48]{1,0:T(4,128)} %param.38) | copy-start | bytes 1732
  652.9 52.7 %copy-start.67 = (f32[3,48]{1,0:T(4,128)S(1)}, f32[3,48]{1,0:T(4,128)}, u32[]{:S(2)}) copy-start(f32[3,48]{1,0:T(4,128)} %param.39) | copy-start | bytes 1732
  652.9 53.3 %copy-start.19 = (bf16[256,1536]{1,0:T(8,128)(2,1)S(1)}, bf16[256,1536]{1,0:T(8,128)(2,1)}, u32[]{:S(2)}) copy-start(bf16[256,1536]{1,0:T(8,128)(2,1)} %param.22) | copy-start | bytes 2359300
  652.9 53.3 %copy-start.25 = (bf16[256,1536]{1,0:T(8,128)(2,1)S(1)}, bf16[256,1536]{1,0:T(8,128)(2,1)}, u32[]{:S(2)}) copy-start(bf16[256,1536]{1,0:T(8,128)(2,1)} %param.23) | copy-start | bytes 2359300
  664.7 74.7 %copy-start.54 = (f32[5,104]{1,0:T(8,128)S(1)}, f32[5,104]{1,0:T(8,128)}, u32[]{:S(2)}) copy-start(f32[5,104]{1,0:T(8,128)} %param.31) | copy-start | bytes 6244
  664.7 74.7 %copy-start.64 = (f32[5,104]{1,0:T(8,128)S(1)}, f32[5,104]{1,0:T(8,128)}, u32[]{:S(2)}) copy-start(f32[5,104]{1,0:T(8,128)} %param.32) | copy-start | bytes 6244
  664.7 74.7 %copy-start.65 = (f32[5,104]{1,0:T(8,128)S(1)}, f32[5,104]{1,0:T(8,128)}, u32[]{:S(2)}) copy-start(f32[5,104]{1,0:T(8,128)} %param.33) | copy-start | bytes 6244
  664.8 447.3 %copy-start.23 = (f32[48,6448]{1,0:T(8,128)S(1)}, f32[48,6448]{1,0:T(8,128)}, u32[]{:S(2)}) copy-start(f32[48,6448]{1,0:T(8,128)} %param.25) | copy-start | bytes 3714052
  (22 other events, 63.6 us)
Sparse Core Ops, SparseCore 0:
  11.5 134.5 all-gather.8
  192.4 7.9 all-gather.12
  228.8 208.9 reduce-scatter.5
  441.1 81.0 all-gather.10
  543.2 8.3 all-gather.14
  619.2 120.1 all-reduce.18
  745.8 366.1 reduce-scatter.3
where the time goes:
time: 1130 us; the launch traced here: 1120 us
  waiting for transfers between devices  739 us (65%)
  matrix products  128 us (11%)
  blocking collectives  126 us (11%)
  other arithmetic  78.4 us (7%)
  local copies, waits for them, and re-layouts  24.1 us (2%)
  between operations  15.7 us (1%)
  starting transfers between devices  12.9 us (1%)
    reduce_scatter x1, waiting for transfers between devices, per_device(): lax.psum_scatter(grad_in_w, ('dp', 'seq'), scatter_dimension=0, tiled=True)  371 us
    reduce_scatter x1, waiting for transfers between devices, per_device(): lax.psum_scatter(grad_out_w, ('dp', 'seq'), scatter_dimension=0, tiled=True)  209 us
    unnamed x2, blocking collectives  83.1 us
    all_gather x1, waiting for transfers between devices, per_device(): lax.all_gather(low_weights[1], ('dp', 'seq'), axis=0, tiled=True)  81.7 us
    all_gather x1, waiting for transfers between devices, per_device(): lax.all_gather(low_weights[0], ('dp', 'seq'), axis=0, tiled=True)  46.6 us
    all_gather x1, blocking collectives, per_device(): lax.all_gather(low_weights[2], ('dp', 'seq'), axis=1, tiled=True)  40.8 us
    dot_general x3, matrix products, block_out(): intra_part = jnp.einsum('htu,uhp->thp', mixing, values, precision=highest)  31.5 us
    unnamed x8, waiting for transfers between devices  30.3 us
  transfers between devices with their start and end apart: 9, of which 5 were waited for; matrix products, arithmetic and copies ran while one was open for 8% of the time, Pallas kernels for 0%

commit v1 on v0

--- a/solution.py
+++ b/solution.py
@@ -1,6 +1,10 @@
+import functools
+
 import jax
 import jax.numpy as jnp
 from jax import lax
+from jax.experimental import pallas as pl
+from jax.experimental.pallas import tpu as pltpu
 from jax.sharding import PartitionSpec as P
 
 D = 1536
@@ -395,6 +399,748 @@
     )
 
 
+MESH_ID = pl.DeviceIdType.MESH
+ANY = pl.BlockSpec(memory_space=pl.ANY)
+PLANES = 4
+QUADS = 4
+RANKS = 8
+
+
+def place():
+    chip = lax.axis_index("dp")
+    return (chip // QUADS, chip % QUADS, lax.axis_index("seq"))
+
+
+def at(plane, quad, core):
+    return (plane * QUADS + quad, core)
+
+
+def flip(core):
+    return 1 - core
+
+
+def xor4(value, k):
+    low, high = value % 2, value // 2
+    if k % 2:
+        low = 1 - low
+    if k // 2:
+        high = 1 - high
+    return 2 * high + low
+
+
+def greet(devices):
+    barrier = pltpu.get_barrier_semaphore()
+    for device in devices:
+        pl.semaphore_signal(barrier, inc=1, device_id=device, device_id_type=MESH_ID)
+    pl.semaphore_wait(barrier, len(devices))
+
+
+def plane_mates(plane, quad, core):
+    mates = []
+    for k in range(QUADS):
+        for other in (core, flip(core)):
+            if not (k == 0 and other is core):
+                mates.append(at(plane, xor4(quad, k), other))
+    return mates
+
+
+def plane_others(plane, quad, core):
+    return [at(xor4(plane, k), quad, core) for k in range(1, PLANES)]
+
+
+class Sems:
+    def __init__(self, send, recv):
+        self.send, self.recv, self.used = (send, recv, 0)
+
+    def copy(self, source, target, device):
+        index = self.used
+        self.used += 1
+        return pltpu.make_async_remote_copy(
+            src_ref=source,
+            dst_ref=target,
+            send_sem=self.send.at[index],
+            recv_sem=self.recv.at[index],
+            device_id=device,
+            device_id_type=MESH_ID,
+        )
+
+
+class PlaneGather:
+    def __init__(self, sems, own, block, plane, quad, core):
+        near_x, near_y, far = (xor4(quad, k) for k in (1, 2, 3))
+        rank = 2 * quad + core
+        rank_x, rank_y, rank_far = (2 * q + core for q in (near_x, near_y, far))
+        to_x, to_y = (at(plane, near_x, core), at(plane, near_y, core))
+        sibling = at(plane, quad, flip(core))
+        whole = [0, 1]
+        self.own = [
+            sems.copy(own(h), block(rank, h), device)
+            for device in (to_x, to_y, sibling)
+            for h in whole
+        ]
+        self.relay_x = [
+            sems.copy(block(rank_x, 0), block(rank_x, 0), to_y),
+        ] + [sems.copy(block(rank_x, h), block(rank_x, h), sibling) for h in whole]
+        self.relay_y = [
+            sems.copy(block(rank_y, 1), block(rank_y, 1), to_x),
+        ] + [sems.copy(block(rank_y, h), block(rank_y, h), sibling) for h in whole]
+        self.relay_far = [
+            sems.copy(block(rank_far, h), block(rank_far, h), sibling) for h in whole
+        ]
+
+    def start(self):
+        for copy in self.own:
+            copy.start()
+
+    def forward(self):
+        self.own[0].wait_recv()
+        self.relay_x[0].start()
+        self.own[3].wait_recv()
+        self.relay_y[0].start()
+        self.own[1].wait_recv()
+        self.own[2].wait_recv()
+        for copy in self.relay_x[1:] + self.relay_y[1:]:
+            copy.start()
+
+    def finish(self):
+        for h, relay in ((0, self.relay_x[0]), (1, self.relay_y[0])):
+            relay.wait_recv()
+            self.relay_far[h].start()
+        for copy in self.own[4:] + self.relay_x[1:] + self.relay_y[1:] + self.relay_far:
+            copy.wait_recv()
+        for copy in self.own + self.relay_x + self.relay_y + self.relay_far:
+            copy.wait_send()
+
+
+class LineGather:
+    def __init__(self, sems, own, block, plane, quad, core):
+        self.plane = plane
+        self.right, self.left = ([], [])
+        for hop in range(PLANES - 1):
+            for copies, step in ((self.right, 1), (self.left, -1)):
+                index = plane - step * hop
+                source = own if hop == 0 else block(index)
+                copies.append(sems.copy(source, block(index), at(plane + step, quad, core)))
+
+    def sends(self, hop, step):
+        if step > 0:
+            return (self.plane - hop >= 0) & (self.plane < PLANES - 1)
+        return (self.plane + hop < PLANES) & (self.plane > 0)
+
+    def receives(self, hop, step):
+        if step > 0:
+            return self.plane - 1 - hop >= 0
+        return self.plane + 1 + hop < PLANES
+
+    def start(self, hop):
+        for copies, step in ((self.right, 1), (self.left, -1)):
+
+            @pl.when(self.sends(hop, step))
+            def go():
+                copies[hop].start()
+
+    def arrive(self, hop):
+        for copies, step in ((self.right, 1), (self.left, -1)):
+
+            @pl.when(self.receives(hop, step))
+            def landed():
+                copies[hop].wait_recv()
+
+    def sent(self):
+        for hop in range(PLANES - 1):
+            for copies, step in ((self.right, 1), (self.left, -1)):
+
+                @pl.when(self.sends(hop, step))
+                def left():
+                    copies[hop].wait_send()
+
+
+def gather_kernel(tok, cot, wz, wc, wo, o_tok, o_cot, o_wz, o_wc, s_wo, o_wo, send, recv, local):
+    plane, quad, core = place()
+    rank = 2 * quad + core
+    sibling = at(plane, quad, flip(core))
+    sems = Sems(send, recv)
+    where = (plane, quad, core)
+    locals_ = []
+
+    def keep(source, target):
+        copy = pltpu.make_async_copy(source, target, local.at[len(locals_)])
+        locals_.append(copy)
+        copy.start()
+        return copy
+
+    half = tok.shape[0] // 2
+    rows = wc.shape[0]
+
+    def token_block(buffer):
+        return lambda r, h: buffer.at[r, pl.ds(h * half, half)]
+
+    def token_own(buffer):
+        return lambda h: buffer.at[pl.ds(h * half, half)]
+
+    line_c = LineGather(sems, wc, lambda q: o_wc.at[q, rank], *where)
+    line_o = LineGather(sems, wo, lambda q: s_wo.at[q], *where)
+    shuffle = []
+    for k in range(1, RANKS):
+        other_core = flip(core) if k % 2 else core
+        other_quad = xor4(quad, k // 2)
+        shuffle.append(
+            sems.copy(wz.at[2 * other_quad + other_core], o_wz.at[plane, rank], at(plane, other_quad, other_core))
+        )
+    halves = [
+        LineGather(
+            sems,
+            o_wz.at[plane, pl.ds(4 * h, 4)],
+            lambda q, h=h: o_wz.at[q, pl.ds(4 * h, 4)],
+            *where,
+        )
+        for h in range(2)
+    ]
+    tokens = PlaneGather(sems, token_own(tok), token_block(o_tok), *where)
+    grads = PlaneGather(sems, token_own(cot), token_block(o_cot), *where)
+    common = PlaneGather(
+        sems,
+        lambda h: o_wc.at[pl.ds(2 * h, 2), rank],
+        lambda r, h: o_wc.at[pl.ds(2 * h, 2), r],
+        *where,
+    )
+    cross_o = [
+        sems.copy(s_wo.at[2 * flip(core) + k], o_wo.at[k, core], sibling) for k in range(2)
+    ]
+
+    greet(plane_mates(*where) + plane_others(*where))
+    line_c.start(0)
+    for copy in shuffle:
+        copy.start()
+    line_o.start(0)
+    tokens.start()
+    own_wz = keep(wz.at[rank], o_wz.at[plane, rank])
+    own_wc = keep(wc, o_wc.at[plane, rank])
+    own_wo = keep(wo, s_wo.at[plane])
+    own_tok = keep(tok, o_tok.at[rank])
+    own_cot = keep(cot, o_cot.at[rank])
+    own_wz.wait()
+    for copy in shuffle:
+        copy.wait_recv()
+    halves[0].start(0)
+    halves[1].start(0)
+    for hop in range(PLANES - 1):
+        line_c.arrive(hop)
+        if hop < PLANES - 2:
+            line_c.start(hop + 1)
+    own_wc.wait()
+    common.start()
+    tokens.forward()
+    grads.start()
+    common.forward()
+    for hop in range(PLANES - 1):
+        for h in range(2):
+            halves[h].arrive(hop)
+            if hop < PLANES - 2:
+                halves[h].start(hop + 1)
+        line_o.arrive(hop)
+        if hop < PLANES - 2:
+            line_o.start(hop + 1)
+        if hop == 0:
+            tokens.finish()
+            common.finish()
+    own_wo.wait()
+    keeps = []
+    for copy in cross_o:
+        copy.start()
+    keeps = [keep(s_wo.at[2 * core + k], o_wo.at[k, core]) for k in range(2)]
+    grads.forward()
+    grads.finish()
+    for copy in cross_o:
+        copy.wait()
+    for copy in shuffle:
+        copy.wait_send()
+    for line in halves + [line_c, line_o]:
+        line.sent()
+    for copy in [own_tok, own_cot] + keeps:
+        copy.wait()
+
+
+def gather_all(tok, cot, wz, wc, wo):
+    bf16 = jnp.bfloat16
+    shapes = (
+        (RANKS,) + tok.shape,
+        (RANKS,) + cot.shape,
+        (PLANES,) + wz.shape,
+        (PLANES, RANKS) + wc.shape,
+        (PLANES,) + wo.shape,
+        (2, 2) + wo.shape,
+    )
+    outs = pl.pallas_call(
+        gather_kernel,
+        out_shape=[jax.ShapeDtypeStruct(s, bf16) for s in shapes],
+        in_specs=[ANY] * 5,
+        out_specs=[ANY] * 6,
+        scratch_shapes=[
+            pltpu.SemaphoreType.DMA((80,)),
+            pltpu.SemaphoreType.DMA((80,)),
+            pltpu.SemaphoreType.DMA((8,)),
+        ],
+        compiler_params=pltpu.CompilerParams(collective_id=0, has_side_effects=True),
+    )(tok, cot, wz, wc, wo)
+    return (outs[0], outs[1], outs[2], outs[3], outs[5])
+
+
+def core_kernel(*refs):
+    count = (len(refs) - 2) // 2
+    sources, targets, (send, recv) = (refs[:count], refs[count : 2 * count], refs[2 * count :])
+    plane, quad, core = place()
+    sibling = at(plane, quad, flip(core))
+    sems = Sems(send, recv)
+    copies = [sems.copy(s.at[flip(core)], t, sibling) for s, t in zip(sources, targets)]
+    greet([sibling])
+    for copy in copies:
+        copy.start()
+    for copy in copies:
+        copy.wait()
+
+
+def core_swap(ident, *arrays):
+    count = len(arrays)
+    return pl.pallas_call(
+        core_kernel,
+        out_shape=[jax.ShapeDtypeStruct(a.shape[1:], a.dtype) for a in arrays],
+        in_specs=[ANY] * count,
+        out_specs=[ANY] * count,
+        scratch_shapes=[pltpu.SemaphoreType.DMA((count,)), pltpu.SemaphoreType.DMA((count,))],
+        compiler_params=pltpu.CompilerParams(collective_id=ident, has_side_effects=True),
+    )(*arrays)
+
+
+def push_kernel(n_quad, n_plane, n_rank, with_out, *refs):
+    count = n_quad + n_plane + n_rank + with_out
+    sources, targets = (refs[:count], refs[count : 2 * count])
+    send, recv, out_send, out_recv, local = refs[2 * count :]
+    plane, quad, core = place()
+    where = (plane, quad, core)
+    rank = 2 * quad + core
+    sems = Sems(send, recv)
+    copies = []
+    peers = []
+    if n_plane or with_out:
+        peers += plane_others(*where)
+    if with_out:
+        peers += [at(xor4(plane, k), quad, flip(core)) for k in range(PLANES)]
+    if n_rank:
+        peers += plane_mates(*where)
+    elif n_quad:
+        peers += [at(plane, xor4(quad, k), core) for k in range(1, QUADS)]
+    index = n_quad
+    for i in range(n_plane):
+        for k in (2, 3, 1):
+            other = xor4(plane, k)
+            copies.append(
+                sems.copy(sources[index + i].at[other], targets[index + i].at[k - 1], at(other, quad, core))
+            )
+    for i in range(n_quad):
+        for k in (3, 1, 2):
+            other = xor4(quad, k)
+            copies.append(sems.copy(sources[i].at[other], targets[i].at[k - 1], at(plane, other, core)))
+    index += n_plane
+    for i in range(n_rank):
+        for k in range(1, RANKS):
+            other_core = flip(core) if k % 2 else core
+            other_quad = xor4(quad, k // 2)
+            copies.append(
+                sems.copy(
+                    sources[index + i].at[2 * other_quad + other_core],
+                    targets[index + i].at[rank],
+                    at(plane, other_quad, other_core),
+                )
+            )
+    index += n_rank
+    greet(peers)
+    for copy in copies:
+        copy.start()
+    if with_out:
+        source, target = (sources[index], targets[index])
+        mine = (plane // 2 == core)
+        for near in range(2):
+            for side in range(2):
+                to_plane = 2 * core + near
+                itself = (to_plane == plane) & (core == side)
+                remote = pltpu.make_async_remote_copy(
+                    src_ref=source.at[near, side],
+                    dst_ref=target.at[plane],
+                    send_sem=out_send.at[2 * near + side],
+                    recv_sem=out_recv.at[plane],
+                    device_id=at(to_plane, quad, side),
+                    device_id_type=MESH_ID,
+                )
+
+                @pl.when(jnp.logical_not(itself))
+                def go():
+                    remote.start()
+
+                @pl.when(itself)
+                def stay():
+                    pltpu.make_async_copy(source.at[near, side], target.at[plane], local).start()
+
+        for origin in range(PLANES):
+            itself = (plane == origin) & mine
+            landing = pltpu.make_async_remote_copy(
+                src_ref=source.at[0, 0],
+                dst_ref=target.at[origin],
+                send_sem=out_send.at[0],
+                recv_sem=out_recv.at[origin],
+                device_id=at(plane, quad, flip(core)),
+                device_id_type=MESH_ID,
+            )
+
+            @pl.when(jnp.logical_not(itself))
+            def arrived():
+                landing.wait_recv()
+
+            @pl.when(itself)
+            def kept():
+                pltpu.make_async_copy(source.at[0, 0], target.at[origin], local).wait()
+
+        for near in range(2):
+            for side in range(2):
+                itself = (2 * core + near == plane) & (core == side)
+
+                @pl.when(jnp.logical_not(itself))
+                def gone():
+                    pltpu.make_async_remote_copy(
+                        src_ref=source.at[near, side],
+                        dst_ref=target.at[plane],
+                        send_sem=out_send.at[2 * near + side],
+                        recv_sem=out_recv.at[plane],
+                        device_id=at(2 * core + near, quad, side),
+                        device_id_type=MESH_ID,
+                    ).wait_send()
+
+    for copy in copies:
+        copy.wait()
+
+
+def push(ident, quads=(), planes=(), ranks=(), out=None):
+    arrays = tuple(quads) + tuple(planes) + tuple(ranks) + (() if out is None else (out,))
+    shapes = (
+        [(QUADS - 1,) + a.shape[1:] for a in quads]
+        + [(PLANES - 1,) + a.shape[1:] for a in planes]
+        + [a.shape for a in ranks]
+        + ([] if out is None else [(PLANES,) + out.shape[2:]])
+    )
+    copies = 3 * len(quads) + 3 * len(planes) + 7 * len(ranks)
+    return pl.pallas_call(
+        functools.partial(push_kernel, len(quads), len(planes), len(ranks), 0 if out is None else 1),
+        out_shape=[jax.ShapeDtypeStruct(s, a.dtype) for s, a in zip(shapes, arrays)],
+        in_specs=[ANY] * len(arrays),
+        out_specs=[ANY] * len(arrays),
+        scratch_shapes=[
+            pltpu.SemaphoreType.DMA((copies,)),
+            pltpu.SemaphoreType.DMA((copies,)),
+            pltpu.SemaphoreType.DMA((4,)),
+            pltpu.SemaphoreType.DMA((4,)),
+            pltpu.SemaphoreType.DMA,
+        ],
+        compiler_params=pltpu.CompilerParams(collective_id=ident, has_side_effects=True),
+    )(*arrays)
+
+
+def owners_kernel(source, target, send, recv):
+    plane, quad, core = place()
+    mine = 2 * (plane * QUADS + quad) + core
+    sems = Sems(send, recv)
+    copies, peers = ([], [])
+    for k in range(1, PLANES * RANKS):
+        other_plane = xor4(plane, k // RANKS)
+        other_quad = xor4(quad, (k % RANKS) // 2)
+        other_core = flip(core) if k % 2 else core
+        device = at(other_plane, other_quad, other_core)
+        peers.append(device)
+        index = 2 * (other_plane * QUADS + other_quad) + other_core
+        copies.append(sems.copy(source.at[index], target.at[mine], device))
+    greet(peers)
+    for copy in copies:
+        copy.start()
+    for copy in copies:
+        copy.wait()
+
+
+def to_owners(ident, array):
+    return pl.pallas_call(
+        owners_kernel,
+        out_shape=jax.ShapeDtypeStruct(array.shape, array.dtype),
+        in_specs=[ANY],
+        out_specs=ANY,
+        scratch_shapes=[
+            pltpu.SemaphoreType.DMA((PLANES * RANKS - 1,)),
+            pltpu.SemaphoreType.DMA((PLANES * RANKS - 1,)),
+        ],
+        compiler_params=pltpu.CompilerParams(collective_id=ident, has_side_effects=True),
+    )(array)
+
+
+def share_kernel(source, target, send, recv):
+    plane, quad, core = place()
+    rank = 2 * quad + core
+    sems = Sems(send, recv)
+    mates = plane_mates(plane, quad, core)
+    copies = [sems.copy(source, target.at[rank], device) for device in mates]
+    greet(mates)
+    for copy in copies:
+        copy.start()
+    for copy in copies:
+        copy.wait()
+
+
+def share(ident, array):
+    return pl.pallas_call(
+        share_kernel,
+        out_shape=jax.ShapeDtypeStruct((RANKS,) + array.shape, array.dtype),
+        in_specs=[ANY],
+        out_specs=ANY,
+        scratch_shapes=[pltpu.SemaphoreType.DMA((RANKS - 1,))] * 2,
+        compiler_params=pltpu.CompilerParams(collective_id=ident, has_side_effects=True),
+    )(array)
+
+
+OWN_HEADS = HEADS // RANKS
+OWN = OWN_HEADS * HDIM
+RUN = OWN // 2
+COMMON = 2 * NST + HEADS
+COMMON_PAD = 384
+GROUP = 2 * BLOCK
+
+
+def pick_runs(array, plane_runs, quad, core):
+    lead = array.shape[:-1]
+    width = array.shape[-1] // (PLANES * QUADS)
+    split = array.reshape(lead + (2, 2, QUADS, width))
+    zero = 0
+    n = len(lead)
+    taken = lax.dynamic_slice(
+        split, (zero,) * n + (core, 0, quad, 0), lead + (1, 2, 1, width)
+    )
+    return taken.reshape(lead + (2 * width,))
+
+
+def put_runs(array, quad, core):
+    lead = array.shape[:-1]
+    width = array.shape[-1] // 2
+    zeros = jnp.zeros(lead + (2, 2, QUADS, width), array.dtype)
+    n = len(lead)
+    full = lax.dynamic_update_slice(
+        zeros, array.reshape(lead + (1, 2, 1, width)), (0,) * n + (core, 0, quad, 0)
+    )
+    return full.reshape(lead + (width * PLANES * QUADS,))
+
+
+def rank_slices(array):
+    rows = array.shape[0]
+    split = array.reshape(rows, 2, 2, QUADS, RUN)
+    return split.transpose(3, 1, 0, 2, 4).reshape(RANKS, rows, OWN)
+
+
+def rank_join(array):
+    rows = array.shape[1]
+    split = array.reshape(QUADS, 2, rows, 2, RUN)
+    return split.transpose(2, 1, 3, 0, 4).reshape(rows, DIN)
+
+
+def mixer_quad(extended, step_raw, conv_par, head_values, live_rows):
+    rows = step_raw.shape[1]
+    preact = conv_par[KCONV][None, None, :]
+    for tap in range(KCONV):
+        preact = preact + conv_par[tap][None, None, :] * extended[:, tap : tap + rows]
+    conv_act = jax.nn.silu(preact)
+    step_size = jax.nn.softplus(step_raw + head_values[0]) * live_rows[:, :, None]
+    logdec = -jnp.exp(head_values[1]) * step_size
+    return (conv_act, step_size, logdec)
+
+
+def two_blocks(values, keys_in, queries, step_size, logdec, skip_gain):
+    start = jnp.zeros((OWN_HEADS, HDIM, NST), jnp.float32)
+    outs = []
+    for k in range(2):
+        rows = slice(k * BLOCK, (k + 1) * BLOCK)
+        out, start = block_full(
+            values[rows], keys_in[rows], queries[rows], step_size[rows], logdec[rows], skip_gain, start
+        )
+        outs.append(out)
+    return jnp.concatenate(outs, axis=0)
+
+
+def per_device_quad(
+    tokens_in,
+    cotangent,
+    seq_lens,
+    in_weight,
+    in_first,
+    in_second,
+    out_weight,
+    out_first,
+    out_second,
+    conv_weight,
+    conv_first,
+    conv_second,
+    gains,
+    gain_first,
+    gain_second,
+    head_params,
+    head_first,
+    head_second,
+):
+    bf16, f32 = (jnp.bfloat16, jnp.float32)
+    plane, quad, core = place()
+    rank = 2 * quad + core
+    rows = in_weight.shape[0]
+    in_low = in_weight.astype(bf16)
+    out_low = out_weight.astype(bf16)
+    wz = jnp.concatenate([rank_slices(in_low[:, :DIN]), rank_slices(in_low[:, DIN : 2 * DIN])], axis=2)
+    first_len = jnp.full((rows, 1), seq_lens[0, 0] - BLOCK).astype(bf16)
+    conv_flat = jnp.pad(conv_weight.reshape(-1), (0, 8)).astype(bf16).reshape(rows, 11)
+    wc = jnp.concatenate(
+        [in_low[:, 2 * DIN :], gains.astype(bf16).reshape(rows, 3), conv_flat, first_len], axis=1
+    )
+    wc = jnp.pad(wc, ((0, 0), (0, COMMON_PAD - wc.shape[1])))
+    tok, cot, w_own, w_com, w_out = gather_all(tokens_in, cotangent, wz, wc, out_low)
+    tok = tok.reshape(RANKS * BLOCK, D)
+    cot = cot.reshape(RANKS * BLOCK, D)
+    w_own = w_own.reshape(D, 2 * OWN)
+    w_out = w_out.reshape(OWN, D)
+    extras = w_com[:, :, :, COMMON:].astype(f32)
+    gain_par = extras[:, :, :, :3].reshape(D + DIN)
+    conv_par = (
+        extras[:, :, :, 3:14].reshape(PLANES * RANKS, 11 * rows)[:, : 5 * 104]
+        .reshape(PLANES * RANKS, 5, 104).transpose(1, 0, 2).reshape(5, CONVC)
+    )
+    lens = lax.dynamic_index_in_dim(extras, plane, 0, False)[::2, 0, 14] + BLOCK
+    w_com = w_com.reshape(D, COMMON_PAD)[:, :COMMON]
+    live = (jnp.arange(GROUP)[None, :] < lens[:, None]).astype(f32)
+    conv_own = jnp.concatenate([pick_runs(conv_par[:, :DIN], 2, quad, core), conv_par[:, DIN:]], axis=1)
+    gain_out = pick_runs(gain_par[D:], 2, quad, core)
+    head_own = pick_runs(head_params, 2, quad, core)
+
+    scaling = lax.rsqrt(jnp.mean(jnp.square(tok.astype(f32)), axis=1, keepdims=True) + norm_eps)
+    normed = (tok.astype(f32) * scaling * gain_par[:D]).astype(bf16)
+    proj_own = jnp.dot(normed, w_own, preferred_element_type=f32)
+    proj_com = jnp.dot(normed, w_com, preferred_element_type=f32)
+    gate_part = proj_own[:, :OWN]
+    conv_in = jnp.concatenate([proj_own[:, OWN:], proj_com[:, : 2 * NST]], axis=1)
+    step_raw = pick_runs(proj_com[:, 2 * NST :], 2, quad, core)
+    extended = jnp.pad(conv_in.reshape(QUADS, GROUP, -1), ((0, 0), (KCONV - 1, 0), (0, 0)))
+    (conv_act, step_size, logdec), pull_mixer = jax.vjp(
+        lambda *a: mixer_quad(*a, live), extended, step_raw.reshape(QUADS, GROUP, OWN_HEADS), conv_own, head_own
+    )
+    used = as_float(conv_act.astype(bf16))
+    values = used[:, :, :OWN].reshape(QUADS, GROUP, OWN_HEADS, HDIM)
+    keys_in = used[:, :, OWN : OWN + NST]
+    queries = used[:, :, OWN + NST :]
+    mixed, pull_ssd = jax.vjp(
+        jax.vmap(two_blocks, in_axes=(0, 0, 0, 0, 0, None)), values, keys_in, queries, step_size, logdec, head_own[2]
+    )
+    mixed = mixed.reshape(RANKS * BLOCK, OWN)
+    out_grad = (cot.astype(f32) * live.reshape(-1, 1)).astype(bf16)
+    grad_normed_out = contract_cols(out_grad, w_out)
+    sig = jax.nn.sigmoid(gate_part)
+    gate_act = gate_part * sig
+    gated = mixed * gate_act
+    weighted = grad_normed_out * gain_out
+    stats = jnp.stack([jnp.sum(gated * gated, axis=1), jnp.sum(weighted * gated, axis=1)])
+    stats = stats.reshape(32, 128)
+    shared = share(1, stats)
+    ranks = lax.broadcasted_iota(jnp.int32, (RANKS, 1, 1), 0)
+    total = jnp.sum(jnp.where(ranks == rank, stats[None], shared), axis=0).reshape(2, RANKS * BLOCK, 1)
+    scale_out = lax.rsqrt(total[0] / DIN + norm_eps)
+    normed_out = (gated * scale_out * gain_out).astype(bf16)
+    branch = jnp.dot(normed_out, w_out, preferred_element_type=f32).astype(bf16)
+    grad_out_w = contract_rows(normed_out, out_grad).astype(bf16)
+    grad_gated = scale_out * weighted - gated * (scale_out**3 * total[1] / DIN)
+    grad_gain_out = jnp.sum(grad_normed_out * gated * scale_out, axis=0)
+    grad_gate = grad_gated * mixed * (sig * (1.0 + gate_part * (1.0 - sig)))
+    mixed_back = as_float((grad_gated * gate_act).astype(bf16))
+    grad_values, grad_keys, grad_queries, grad_step, grad_logdec, grad_skip = pull_ssd(
+        mixed_back.reshape(QUADS, GROUP, OWN_HEADS, HDIM)
+    )
+    grad_act = jnp.concatenate([grad_values.reshape(QUADS, GROUP, OWN), grad_keys, grad_queries], axis=2)
+    grad_ext, grad_raw, grad_conv_own, grad_head_own = pull_mixer((grad_act, grad_step, grad_logdec))
+    grad_conv_in = grad_ext[:, KCONV - 1 :].reshape(RANKS * BLOCK, OWN + 2 * NST)
+    grad_proj_own = jnp.concatenate([grad_gate, grad_conv_in[:, :OWN]], axis=1).astype(bf16)
+    grad_raw = put_runs(grad_raw.reshape(RANKS * BLOCK, OWN_HEADS), quad, core)
+    grad_proj_com = jnp.concatenate([grad_conv_in[:, OWN:], grad_raw], axis=1).astype(bf16)
+    grad_normed = (contract_cols(grad_proj_own, w_own) + contract_cols(grad_proj_com, w_com)).astype(bf16)
+    grad_own_w = contract_rows(normed, grad_proj_own).astype(bf16)
+    grad_com_w = jnp.pad(contract_rows(normed, grad_proj_com), ((0, 0), (0, COMMON_PAD - COMMON))).astype(bf16)
+
+    def by_core(array, lead):
+        split = array.reshape((lead, 2) + array.shape[1:]) if array.shape[0] == 2 * lead else array
+        return jnp.moveaxis(split, 1, 0)
+
+    parts = (
+        by_core(branch.reshape(RANKS, BLOCK, D), QUADS),
+        by_core(grad_normed.reshape(RANKS, BLOCK, D), QUADS),
+        by_core(grad_com_w.reshape(PLANES * QUADS * 2, rows, COMMON_PAD), PLANES * QUADS),
+    )
+    swapped = core_swap(2, *parts)
+
+    def own_part(array, index):
+        return lax.dynamic_index_in_dim(array, index, 0, False)
+
+    sums = [
+        (own_part(a, core).astype(f32) + b.astype(f32)).astype(bf16) for a, b in zip(parts, swapped)
+    ]
+    sums[2] = sums[2].reshape(PLANES, QUADS, rows, COMMON_PAD).transpose(1, 0, 2, 3)
+    own_blocks = grad_own_w.reshape(PLANES, RANKS, rows, 2 * OWN)
+    got = push(
+        3,
+        quads=sums,
+        planes=(own_blocks,),
+        out=grad_out_w.reshape(2, 2, out_weight.shape[0], D),
+    )
+
+    def add_up(own, index, others):
+        return own_part(own, index).astype(f32) + jnp.sum(others.astype(f32), axis=0)
+
+    branch_sum = add_up(sums[0], quad, got[0])
+    normed_sum = add_up(sums[1], quad, got[1])
+    com_sum = add_up(sums[2], quad, got[2]).astype(bf16)
+    own_sum = add_up(own_blocks, plane, got[3]).astype(bf16)
+    out_sum = jnp.sum(got[4].astype(f32), axis=0)
+    com_got, own_got = push(4, planes=(com_sum,), ranks=(own_sum,))
+    com_total = add_up(com_sum, plane, com_got)
+    own_all = jnp.where(ranks == rank, own_sum, own_got).astype(f32)
+    in_sum = jnp.concatenate(
+        [rank_join(own_all[:, :, :OWN]), rank_join(own_all[:, :, OWN:]), com_total[:, :COMMON]], axis=1
+    )
+
+    token_rows = tokens_in.astype(f32)
+    own_live = lax.dynamic_slice(live, (quad, core * BLOCK), (1, BLOCK)).reshape(BLOCK, 1)
+    mixed_out = (token_rows + own_live * branch_sum).astype(bf16)
+    normed_value, pull_pre = jax.vjp(pre_norm, token_rows, gain_par[:D])
+    grad_rows, grad_gain_pre = pull_pre(normed_sum)
+    grad_input = cotangent.astype(f32) + grad_rows
+
+    grad_gains = jnp.concatenate([grad_gain_pre, put_runs(grad_gain_out, quad, core)]).reshape(32, 144)
+    grad_conv = jnp.concatenate(
+        [put_runs(grad_conv_own[:, :OWN], quad, core), grad_conv_own[:, OWN:]], axis=1
+    ).reshape(5, 32, 104).transpose(1, 0, 2).reshape(32, 520)
+    grad_head_own = grad_head_own + jnp.stack([jnp.zeros_like(grad_skip), jnp.zeros_like(grad_skip), grad_skip])
+    grad_head = jnp.broadcast_to(put_runs(grad_head_own, quad, core).reshape(1, 144), (32, 144))
+    small = jnp.concatenate([grad_gains, grad_conv, grad_head, jnp.zeros((32, 216), f32)], axis=1)
+    small = small.reshape(32, 8, 128)
+    small_got = to_owners(5, small)
+    mine = rank + RANKS * plane
+    owners = lax.broadcasted_iota(jnp.int32, (32, 1, 1), 0)
+    small_sum = jnp.sum(jnp.where(owners == mine, small, small_got), axis=0).reshape(-1)
+    gain_sum = small_sum[:144]
+    conv_sum = small_sum[144:664].reshape(5, 104)
+    head_sum = small_sum[664:808].reshape(3, 48)
+    new_in = adam_update(in_weight, in_first, in_second, in_sum, rate_in)
+    new_out = adam_update(out_weight, out_first, out_second, out_sum, rate_out)
+    new_conv = adam_update(conv_weight, conv_first, conv_second, conv_sum, rate_conv)
+    new_gain = adam_update(gains, gain_first, gain_second, gain_sum, rate_gain)
+    new_head = adam_update(head_params, head_first, head_second, head_sum, rate_head)
+    return (mixed_out, grad_input) + new_in + new_out + new_conv + new_gain + new_head
+
+
 def solution(mesh):
     placed = (
         P(("dp", "seq"), None),
@@ -416,8 +1162,9 @@
         P(),
         P(),
     )
+    quad = dict(mesh.shape) == {"dp": PLANES * QUADS, "seq": 2}
     return jax.shard_map(
-        per_device,
+        per_device_quad if quad else per_device,
         mesh=mesh,
         in_specs=placed,
         out_specs=(

time: 1130 us -> 591 us (0.52)
  waiting for transfers between devices: 739 us -> 0 us
  Pallas kernels: 0 us -> 222 us
  blocking collectives: 126 us -> 0 us
  local copies, waits for them, and re-layouts: 24.1 us -> 92.5 us
  other arithmetic: 78.4 us -> 135 us
  between operations: 15.7 us -> 2.63 us
  starting transfers between devices: 12.9 us -> 0 us
    reduce_scatter x2 -> x0, waiting for transfers between devices: 580 us -> none  [the longest x1 371 us: per_device(): lax.psum_scatter(grad_in_w, ('dp', 'seq'), scatter_dimension=0, tiled=True)]
    pallas_call x0 -> x6, Pallas kernels: none -> 222 us  [the longest x1 105 us: gather_all(): pl.pallas_call(gather_kernel, out_shape=[jax.ShapeDtypeStruct(s, bf16) fo...]
    all_gather x4 -> x0, waiting for transfers between devices: 128 us -> none  [the longest x1 81.7 us: per_device(): lax.all_gather(low_weights[1], ('dp', 'seq'), axis=0, tiled=True)]
    unnamed x2 -> x0, blocking collectives: 83.1 us -> none
    all_gather x2 -> x0, blocking collectives: 42.8 us -> none  [the longest x1 40.8 us: per_device(): lax.all_gather(low_weights[2], ('dp', 'seq'), axis=1, tiled=True)]
    convert_element_type x8 -> x16, other arithmetic: 15.9 us -> 47.5 us  [the longest x2 17.1 us: per_device_quad(): out_grad = (cot.astype(f32) * live.reshape(-1, 1)).astype(bf16)]
    unnamed x8 -> x0, waiting for transfers between devices: 30.3 us -> none
    reshape x6 -> x34, local copies, waits for them, and re-layouts: 0.15 us -> 29.7 us  [the longest x1 6.13 us: per_device_quad(): conv_in.reshape(QUADS, GROUP, -1)]
  transfers between devices with their start and end apart: 9 -> 0, of which waited for: 5 -> 0; matrix products, arithmetic and copies ran while one was open for 8% -> 0% of each run, Pallas kernels for 0% -> 0%
where the time goes in v1:
time: 591 us; the launch traced here: 585 us
  Pallas kernels  222 us (38%)
  other arithmetic  135 us (23%)
  matrix products  133 us (23%)
  local copies, waits for them, and re-layouts  92.5 us (16%)
    pallas_call x1, Pallas kernels, gather_all(): pl.pallas_call(gather_kernel, out_shape=[jax.ShapeDtypeStruct(s, bf16) fo...  105 us
    pallas_call x2, Pallas kernels, push(): pl.pallas_call(functools.partial(push_kernel, len(quads), len(planes), le...  89.3 us
    dot_general x6, matrix products, block_out(): intra_part = jnp.einsum('htu,uhp->thp', mixing, values, precision=highest)  34 us
    dot_general x3, matrix products, contract_cols(): lax.dot_general(left, right, (((1,), (1,)), ((), ())), preferred_element_...  27.2 us
    dot_general x3, matrix products, contract_rows(): lax.dot_general(left, right, (((0,), (0,)), ((), ())), preferred_element_...  21.7 us
    unnamed x200, local copies, waits for them, and re-layouts  19 us
    convert_element_type x2, other arithmetic, per_device_quad(): out_grad = (cot.astype(f32) * live.reshape(-1, 1)).astype(bf16)  17.1 us
    another operation x3, other arithmetic  14.6 us

profile of v1, /device:TPU:0, one launch (start us, length us, event | category | flops | bytes accessed | tf_op | source)
XLA Modules:
  0.0 584.6 jit_solution(8654788442950804615)
XLA Ops:
  7.1 105.2 %shard_map.305 = (bf16[8,256,1536]{2,1,0:T(8,128)(2,1)}, bf16[8,256,1536]{2,1,0:T(8,128)(2,1)}, bf16[4,8,48,768]{3,2,1,0:T(8,128)(2,1)}, bf16[4,8,48,384]{3,2,1,...) custom-call(bf16[256,1536]{1,0:T(8,128)(2,1)} %tok.1, bf16[256,1536]{1,0:T(8,128)(2,1)} %cot.1, ...), custom_call_target="tpu_custom_call" | custom-call | tf_op jit(solution)/shard_map/pallas_call | solution.py:674
  114.3 4.2 multiply_reduce_fusion
  118.9 7.7 %fusion = (bf16[2048,1536]{1,0:T(8,128)(2,1)}, bf16[2048,1536]{1,0:T(8,128)(2,1)S(1)}) fusion(f32[2048]{0:T(1024)S(1)} %bitcast.310, bf16[8,256,1536]{2,1,0:T(8,128)(2,1)} %get-tuple-element.35, f32[1536]{0:T(1024)S(1)} %slice.250, f32[2048]{0:T(1024)S(1)} %bitcast.311, bf16[8,256,1536]{2,1,0:T(8,128)(2,1)S(1)} %copy-done), kind=kLoop, calls=%fused_computation.1 | loop fusion | flops 22020096 | bytes 25188352 | tf_op jit(solution)/shard_map/convert_element_type | solution.py:1041
  126.6 2.2 fusion.102
  137.5 9.4 %multiply_convert_fusion = (bf16[8,256,1536]{2,1,0:T(8,128)(2,1)}, bf16[8,256,1536]{2,1,0:T(8,128)(2,1)S(1)}) fusion(f32[8,256]{1,0:T(8,128)S(1)} %compare_convert_fusion, bf16[8,256,1536]{2,1,0:T(8,128)(2,1)} %get-tuple-element.35, f32[1536]{0:T(1024)S(1)} %slice.250, f32[8,256]{1,0:T(8,128)S(1)} %get-tuple-element.140, ...), kind=kLoop, calls=%fused_computation.6 | loop fusion | flops 22020096 | bytes 25188352 | tf_op jit(solution)/shard_map/convert_element_type | solution.py:1041
  146.9 5.4 fusion.209
  152.6 2.5 copy-done.16
  155.4 2.6 pad_maximum_fusion
  158.1 6.1 %copy.331 = f32[2048,640]{1,0:T(8,128)} copy(f32[2048,640]{0,1:T(8,128)} %pad_maximum_fusion) | data formatting | bytes 10485760 | tf_op jit(solution)/shard_map/reshape | solution.py:1029
  165.4 12.5 %multiply_convert_fusion.2 = (bf16[4,512,640]{2,1,0:T(8,128)(2,1)S(1)}, f32[4,512,640]{2,1,0:T(8,128)}) fusion(f32[4,512,640]{2,1,0:T(8,128)} %bitcast.258, f32[640]{0:T(1024)S(1)} %get-tuple-element.84, f32[640]{0:T(1024)S(1)} %get-tuple-element.81, f32[640]{0:T(1024)S(1)} %get-tuple-element.82, f32[640]{0:T(1024)S(1)} %get-tuple-element.83, ...), kind=kLoop, calls=%fused_computation.43 | loop fusion | flops 17039360 | bytes 13120000 | tf_op jit(solution)/shard_map/convert_element_type | solution.py:1033
  179.3 2.6 copy.261
  181.9 3.5 reshape.557
  188.7 7.9 %fusion.59 = f32[4,256,6,64]{1,3,2,0:T(8,128)} fusion(f32[4,256,6,64]{1,3,2,0:T(8,128)} %fusion.124, f32[4,6,256]{2,1,0:T(8,128)S(1)} %copy.265, f32[4,6,256]{2,1,0:T(8,128)S(1)} %bitcast.301, f32[4,256,256]{2,1,0:T(8,128)} %fusion.145, pred[256,256]{1,0:T(8,128)(4,1)S(1)} %convert_compare_fusion, f32[4,512,6,64]{1,3,2,0:T(8,128)} %reshape.557, ...), kind=kOutput, calls=%fused_computation.125 | convolution fusion | flops 1215823872 | bytes 6750720 | tf_op jit(solution)/shard_map/jvp(vmap(htu,uhp->thp))/dot_general | solution.py:158
  198.5 2.3 fusion.78
  207.8 6.9 %fusion.58 = f32[4,256,6,64]{1,3,2,0:T(8,128)S(1)} fusion(f32[4,256,6,64]{1,3,2,0:T(8,128)} %fusion.127, f32[4,6,256]{2,1,0:T(8,128)} %copy.267, f32[4,6,256]{2,1,0:T(8,128)S(1)} %bitcast.307, f32[4,256,256]{2,1,0:T(8,128)S(1)} %fusion.141, pred[256,256]{1,0:T(8,128)(4,1)} %copy-done.53, f32[4,512,6,64]{1,3,2,0:T(8,128)} %reshape.557, ...), kind=kOutput, calls=%fused_computation.123 | convolution fusion | flops 1215823872 | bytes 6750720 | tf_op jit(solution)/shard_map/jvp(vmap(htu,uhp->thp))/dot_general | solution.py:158
  217.1 3.1 copy.336
  220.8 10.8 %multiply_reduce_fusion.11 = (f32[2048]{0:T(1024)S(1)}, f32[2048]{0:T(1024)S(1)}, f32[2048,384]{0,1:T(8,128)}, f32[2048,384]{0,1:T(8,128)}) fusion(f32[384]{0:T(512)S(1)} %mul.741, f32[2048,384]{0,1:T(8,128)} %bitcast.271, f32[2048,768]{0,1:T(8,128)} %copy-done.16, bf16[2048,1536]{1,0:T(8,128)(2,1)} %bitcast.284, bf16[384,1536]{1,0:T(8,128)(2,1)} %bitcast.321), kind=kOutput, calls=%fused_computation.65 | convolution fusion | flops 2423779328 | bytes 20071936 | tf_op jit(solution)/shard_map/dot_general | solution.py:197
  232.2 5.6 shard_map.306
  239.5 6.7 %multiply_convert_fusion.4 = (bf16[2048,384]{0,1:T(8,128)(2,1)}, bf16[2048,384]{0,1:T(8,128)(2,1)}, f32[384]{0:T(512)}) fusion(f32[2048,384]{0,1:T(8,128)S(1)} %bitcast.272, f32[2048,768]{0,1:T(8,128)} %copy-done.16, f32[2048,384]{0,1:T(8,128)} %get-tuple-element.105, f32[2048]{0:T(1024)S(1)} %fusion.165, f32[2048,384]{0,1:T(8,128)} %get-tuple-element.145, ...), kind=kLoop, calls=%fused_computation.61 | loop fusion | flops 15728256 | bytes 15748096 | tf_op jit(solution)/shard_map/convert.20
  246.1 4.2 reshape.560
  250.4 2.2 fusion.203
  252.6 3.1 multiply_reduce_fusion.18
  255.7 4.6 multiply_reduce_fusion.12
  262.4 10.0 %fusion.21 = (f32[4,6,256]{2,1,0:T(8,128)S(1)}, f32[4,6,256]{2,1,0:T(8,128)S(1)}, f32[4,6,256]{2,1,0:T(8,128)}, f32[4,256,256]{2,1,0:T(8,128)}, f32[4,256,256]{2...) fusion(f32[4,6,256]{2,1,0:T(8,128)S(1)} %copy-done.62, ...), kind=kOutput, calls=%fused_computation.51 | convolution fusion | flops 241659904 | bytes 12468224 | tf_op jit(solution)/shard_map/transpose(jvp(vmap(htu,uhp->thp)))/dot_general | solution.py:158
  275.8 2.7 fusion.199
  285.7 2.1 add_bitcast_fusion
  289.6 6.5 %fusion.194 = (f32[6]{0:T(128)}, bf16[4,512,6]{2,0,1:T(4,128)(2,1)}, f32[6]{0:T(128)}) fusion(f32[4,512,6]{2,0,1:T(4,128)} %copy-done.10, f32[6]{0:T(128)} %copy-done.77, f32[4,512]{0,1:T(8,128)S(1)} %copy-done.28, f32[4,256,6]{2,0,1:T(4,128)} %add_bitcast_fusion, f32[4,256,6]{2,0,1:T(4,128)} %bitcast.293, f32[6]{0:T(128)} %copy-done.78, ...), kind=kLoop, calls=%fused_computation.344 | loop fusion | flops 270324 | bytes 229472 | tf_op jit(solution)/shard_map/transpose(jvp())/reduce_sum | solution.py:954
  299.3 7.6 %convolution_convert_fusion.2 = bf16[384,1536]{1,0:T(8,128)(2,1)} fusion(bf16[2048,1536]{1,0:T(8,128)(2,1)} %get-tuple-element.149, f32[2048,384]{0,1:T(8,128)} %get-tuple-element.105, f32[2048]{0:T(1024)} %copy-done.57, f32[384]{0:T(512)} %copy-done.69), kind=kOutput, calls=%fused_computation.100 | convolution fusion | flops 2418868224 | bytes 10626560 | tf_op jit(solution)/shard_map/dot_general | solution.py:191
  306.9 4.0 bitcast_add_fusion.1
  310.9 4.2 fusion.57
  315.1 2.0 pad_add_fusion.3
  317.1 3.8 copy.288
  320.9 2.4 fusion.148
  323.3 4.4 fusion.83
  327.8 2.2 convolution_add_fusion.2
  330.1 2.8 fusion.86
  334.7 2.7 fusion.89
  339.1 5.9 %multiply_reduce_fusion.8 = (f32[640]{0:T(1024)S(1)}, f32[640]{0:T(1024)S(1)}, f32[640]{0:T(1024)S(1)}, f32[640]{0:T(1024)S(1)}, f32[640]{0:T(1024)S(1)}, /*index=5*/f32[4,512,640]{2,1,0:T(8,128)}) fusion(f32[2048,640]{1,0:T(8,128)S(1)} %bitcast.260, f32[4,512,640]{2,1,0:T(8,128)S(1)} %bitcast.261, f32[4,512,640]{2,1,0:T(8,128)S(1)} %bitcast.268, ...), kind=kLoop, calls=%fused_computation.42 | loop fusion | flops 26211200 | bytes 26227200 | tf_op jit(solution)/shard_map/transpose(jvp())/reduce_sum | solution.py:952
  345.0 9.9 %broadcast_multiply_fusion = (f32[4,512,640]{2,1,0:T(8,128)}, f32[4,512,640]{2,1,0:T(8,128)}, f32[4,512,640]{2,1,0:T(8,128)}, f32[4,512,640]{2,1,0:T(8,128)}) fusion(f32[4,512,640]{2,1,0:T(8,128)} %get-tuple-element.96, f32[640]{0:T(1024)S(1)} %get-tuple-element.84, f32[640]{0:T(1024)S(1)} %get-tuple-element.83, f32[640]{0:T(1024)S(1)} %get-tuple-element.82, ...), kind=kLoop, calls=%fused_computation.102 | loop fusion | flops 5242880 | bytes 26224640 | tf_op jit(solution)/shard_map/transpose(jvp())/mul | solution.py:952
  354.9 7.9 %fusion.19 = bf16[4,512,640]{2,1,0:T(8,128)(2,1)S(1)} fusion(f32[4,512,640]{2,1,0:T(8,128)} %get-tuple-element.118, f32[4,512,640]{2,1,0:T(8,128)} %get-tuple-element.119, f32[4,512,640]{2,1,0:T(8,128)} %get-tuple-element.120, f32[4,512,640]{2,1,0:T(8,128)} %get-tuple-element.117), kind=kLoop, calls=%fused_computation.34 | loop fusion | flops 5242880 | bytes 23592960 | tf_op jit(solution)/shard_map/convert.22
  364.1 2.7 copy.332
  366.8 9.2 %convolution_convert_fusion.1 = bf16[1536,768]{1,0:T(8,128)(2,1)} fusion(bf16[2048,1536]{1,0:T(8,128)(2,1)} %copy-done.19, bf16[2048,384]{0,1:T(8,128)(2,1)} %copy.332, bf16[2048,384]{0,1:T(8,128)(2,1)} %get-tuple-element.110), kind=kOutput, calls=%fused_computation.55 | convolution fusion | flops 4839309312 | bytes 11796480 | tf_op jit(solution)/shard_map/dot_general | solution.py:191
  379.3 4.9 convolution_convert_fusion.3
  387.2 9.8 %fusion.49 = f32[2048,1536]{1,0:T(8,128)} fusion(bf16[1536,768]{1,0:T(8,128)(2,1)} %bitcast.319, bf16[2048,384]{0,1:T(8,128)(2,1)S(1)} %copy-done.37, bf16[2048,384]{0,1:T(8,128)(2,1)S(1)} %copy-done.35), kind=kOutput, calls=%fused_computation.108 | convolution fusion | flops 4838129664 | bytes 18087936 | tf_op jit(solution)/shard_map/dot_general | solution.py:197
  396.9 6.7 %add_convert_fusion = bf16[2048,1536]{1,0:T(8,128)(2,1)S(1)} fusion(f32[2048,1536]{1,0:T(8,128)} %fusion.49, bf16[1536,384]{1,0:T(8,128)(2,1)S(1)} %bitcast.296, bf16[2048,48]{0,1:T(8,128)(2,1)S(1)} %reshape.564, bf16[2048,256]{0,1:T(8,128)(2,1)S(1)} %copy.333), kind=kOutput, calls=%fused_computation.5 | convolution fusion | flops 1921384448 | bytes 21299200 | tf_op jit(solution)/shard_map/dot_general | solution.py:197
  403.7 3.6 copy.355
  408.0 3.9 convolution_convert_fusion
  411.9 3.3 copy.356
  415.3 11.4 %shard_map.307 = (bf16[4,256,1536]{2,1,0:T(8,128)(2,1)}, bf16[4,256,1536]{2,1,0:T(8,128)(2,1)}, bf16[16,48,384]{2,1,0:T(8,128)(2,1)}) custom-call(bf16[2,4,256,1536]{3,2,1,0:T(8,128)(2,1)} %bitcast.263, bf16[2,4,256,1536]{3,2,1,0:T(8,128)(2,1)} %bitcast.262, bf16[2,16,48,384]{3,2,1,0:T(8,128)(2,1)} %bitcast.282), custom_call_target="tpu_custom_call" | custom-call | tf_op jit(solution)/shard_map/pallas_call | solution.py:705
  428.9 5.5 fusion.3.refs_1_
  434.5 2.6 fusion.4.refs_0_
  437.1 78.5 %shard_map.308 = (bf16[3,256,1536]{2,1,0:T(8,128)(2,1)}, bf16[3,256,1536]{2,1,0:T(8,128)(2,1)}, bf16[3,4,48,384]{3,2,1,0:T(8,128)(2,1)}, bf16[3,8,48,768]{3,2,1,0:T(8,128)(2,1)}, bf16[4,96,1536]{2,1,0:T(8,128)(2,1)}) custom-call(bf16[4,256,1536]{2,1,0:T(8,128)(2,1)} %fusion.4.refs_0_, bf16[4,256,1536]{2,1,0:T(8,128)(2,1)} %fusion.3.refs_1_, ...), custom_call_target="tpu_custom_call" | custom-call | tf_op jit(solution)/shard_map/pallas_call | solution.py:831
  515.6 2.4 convert_reduce_fusion
  521.9 10.1 %shard_map.310 = f32[32,8,128]{2,1,0:T(8,128)} custom-call(f32[32,8,128]{2,1,0:T(8,128)} %bitcast.300), custom_call_target="tpu_custom_call" | custom-call | tf_op jit(solution)/shard_map/pallas_call | solution.py:868
  537.1 2.0 fusion.96.refs_1_
  540.8 10.9 %shard_map.309 = (bf16[3,48,384]{2,1,0:T(8,128)(2,1)}, bf16[8,48,768]{2,1,0:T(8,128)(2,1)}) custom-call(bf16[4,48,384]{2,1,0:T(8,128)(2,1)} %fusion.123.refs_0_, bf16[8,48,768]{2,1,0:T(8,128)(2,1)} %fusion.96.refs_1_), custom_call_target="tpu_custom_call" | custom-call | tf_op jit(solution)/shard_map/pallas_call | solution.py:831
  554.2 2.5 reshape.568
  556.7 2.5 copy.307
  559.2 2.7 reshape.569
  561.9 2.5 reshape.570
  564.4 2.5 copy.308
  566.9 2.7 reshape.571
  570.4 5.0 multiply_subtract_fusion.1
  577.7 4.9 fusion.50
  (374 shorter events, 86.7 us)
Async XLA Ops:
  2.2 4.2 copy-start.30
  113.8 18.6 %copy-start.56 = (f32[4,512]{1,0:T(4,128)}, f32[4,512]{1,0:T(4,128)S(1)}, u32[]{:S(2)}) copy-start(f32[4,512]{1,0:T(4,128)S(1)} %get-tuple-element.144) | copy-start | bytes 24580
  114.3 23.2 %copy-start.48 = (f32[1536]{0:T(1024)}, f32[1536]{0:T(1024)S(1)}, u32[]{:S(2)}) copy-start(f32[1536]{0:T(1024)S(1)} %slice.250) | copy-start | bytes 18436
  114.3 4.6 copy-start
  118.9 7.7 %copy-start.33 = (bf16[4,8,48,384]{3,2,1,0:T(8,128)(2,1)S(1)}, bf16[4,8,48,384]{3,2,1,0:T(8,128)(2,1)}, u32[]{:S(2)}) copy-start(bf16[4,8,48,384]{3,2,1,0:T(8,128)(2,1)} %get-tuple-element.32) | copy-start | bytes 3538948
  126.6 4.8 copy-start.71
  131.4 4.1 copy-start.10
  137.2 51.4 %copy-start.59 = (f32[4,6,256]{2,1,0:T(8,128)}, f32[4,6,256]{2,1,0:T(8,128)S(1)}, u32[]{:S(2)}) copy-start(f32[4,6,256]{2,1,0:T(8,128)S(1)} %copy.265) | copy-start | bytes 73732
  137.5 9.4 %copy-start.85 = (bf16[4,8,48,768]{3,2,1,0:T(8,128)(2,1)S(1)}, bf16[4,8,48,768]{3,2,1,0:T(8,128)(2,1)}, u32[]{:S(2)}) copy-start(bf16[4,8,48,768]{3,2,1,0:T(8,128)(2,1)} %get-tuple-element.34) | copy-start | bytes 7077892
  177.8 27.6 %copy-start.1 = (bf16[4,512,640]{2,1,0:T(8,128)(2,1)}, bf16[4,512,640]{2,1,0:T(8,128)(2,1)S(1)}, u32[]{:S(2)}) copy-start(bf16[4,512,640]{2,1,0:T(8,128)(2,1)S(1)} %get-tuple-element.108) | copy-start | bytes 7864324
  188.5 8.1 %copy-start.50 = (f32[4,256,6]{1,2,0:T(8,128)}, f32[4,256,6]{1,2,0:T(8,128)S(1)}, u32[]{:S(2)}) copy-start(f32[4,256,6]{1,2,0:T(8,128)S(1)} %exponential_bitcast_fusion.1) | copy-start | bytes 73732
  188.6 8.0 %copy-start.88 = (f32[6]{0:T(128)}, f32[6]{0:T(128)S(1)}, u32[]{:S(2)}) copy-start(f32[6]{0:T(128)S(1)} %mul.720) | copy-start | bytes 76
  188.7 7.9 %copy-start.53 = (pred[256,256]{1,0:T(8,128)(4,1)}, pred[256,256]{1,0:T(8,128)(4,1)S(1)}, u32[]{:S(2)}) copy-start(pred[256,256]{1,0:T(8,128)(4,1)S(1)} %convert_compare_fusion) | copy-start | bytes 196612
  207.8 6.9 %copy-start.38 = (f32[4,256,6,64]{1,3,2,0:T(8,128)S(1)}, f32[4,256,6,64]{1,3,2,0:T(8,128)}, u32[]{:S(2)}) copy-start(f32[4,256,6,64]{1,3,2,0:T(8,128)} %fusion.59) | copy-start | bytes 4718596
  220.8 18.7 %copy-start.69 = (f32[384]{0:T(512)}, f32[384]{0:T(512)S(1)}, u32[]{:S(2)}) copy-start(f32[384]{0:T(512)S(1)} %mul.741) | copy-start | bytes 4612
  220.8 18.7 %copy-start.6 = (f32[48,8,4,512]{3,1,2,0:T(8,128)S(1)}, f32[48,8,4,512]{3,1,2,0:T(8,128)}, u32[]{:S(2)}) copy-start(f32[48,8,4,512]{3,1,2,0:T(8,128)} %copy.336) | copy-start | bytes 9437188
  239.4 6.7 %copy-start.57 = (f32[2048]{0:T(1024)}, f32[2048]{0:T(1024)S(1)}, u32[]{:S(2)}) copy-start(f32[2048]{0:T(1024)S(1)} %fusion.168) | copy-start | bytes 24580
  250.4 5.4 copy-start.2
  250.4 5.4 copy-start.17
  250.4 5.4 copy-start.18
  252.6 9.4 %copy-start.23 = (bf16[4,512,6,64]{1,3,2,0:T(8,128)(2,1)}, bf16[4,512,6,64]{1,3,2,0:T(8,128)(2,1)S(1)}, u32[]{:S(2)}) copy-start(bf16[4,512,6,64]{1,3,2,0:T(8,128)(2,1)S(1)} %get-tuple-element.121) | copy-start | bytes 4718596
  255.7 4.6 copy-start.13
  255.7 5.1 copy-start.9
  278.5 11.1 %copy-start.28 = (f32[4,512]{0,1:T(8,128)S(1)}, f32[4,512]{0,1:T(8,128)}, u32[]{:S(2)}) copy-start(f32[4,512]{0,1:T(8,128)} %copy-done.27) | copy-start | bytes 24580
  299.2 7.6 %copy-start.24 = (bf16[4,512,6,64]{1,3,2,0:T(8,128)(2,1)S(1)}, bf16[4,512,6,64]{1,3,2,0:T(8,128)(2,1)}, u32[]{:S(2)}) copy-start(bf16[4,512,6,64]{1,3,2,0:T(8,128)(2,1)} %copy-done.23) | copy-start | bytes 4718596
  299.2 7.6 %copy-start.44 = (f32[4,256,256]{2,1,0:T(8,128)S(1)}, f32[4,256,256]{2,1,0:T(8,128)}, u32[]{:S(2)}) copy-start(f32[4,256,256]{2,1,0:T(8,128)} %copy-done.42) | copy-start | bytes 3145732
  299.2 7.6 %copy-start.55 = (pred[256,256]{1,0:T(8,128)(4,1)S(1)}, pred[256,256]{1,0:T(8,128)(4,1)}, u32[]{:S(2)}) copy-start(pred[256,256]{1,0:T(8,128)(4,1)} %copy-done.53) | copy-start | bytes 196612
  299.2 7.6 %copy-start.63 = (f32[4,6,256]{2,1,0:T(8,128)S(1)}, f32[4,6,256]{2,1,0:T(8,128)}, u32[]{:S(2)}) copy-start(f32[4,6,256]{2,1,0:T(8,128)} %copy.267) | copy-start | bytes 73732
  299.3 7.6 %copy-start.89 = (f32[6]{0:T(128)S(1)}, f32[6]{0:T(128)}, u32[]{:S(2)}) copy-start(f32[6]{0:T(128)} %copy-done.88) | copy-start | bytes 76
  306.9 4.0 copy-start.36
  320.9 6.9 %copy-start.22 = (f32[4,256,256]{2,1,0:T(8,128)S(1)}, f32[4,256,256]{2,1,0:T(8,128)}, u32[]{:S(2)}) copy-start(f32[4,256,256]{2,1,0:T(8,128)} %get-tuple-element.72) | copy-start | bytes 3145732
  323.3 6.8 %copy-start.15 = (f32[4,6,64,128]{3,2,1,0:T(8,128)S(1)}, f32[4,6,64,128]{3,2,1,0:T(8,128)}, u32[]{:S(2)}) copy-start(f32[4,6,64,128]{3,2,1,0:T(8,128)} %copy-done.14) | copy-start | bytes 2359300
  327.8 5.1 copy-start.21
  327.8 11.2 %slice-start.4 = ((s8[5242880]{0:T(1024)(128)(4,1)}), s8[4194304]{0:T(1024)(128)(4,1)S(1)}, s32[]{:S(2)}) async-start(s8[5242880]{0:T(1024)(128)(4,1)} %bitcast.267), calls=%async_computation.4 | async-start | bytes 8388608
  330.0 9.0 %slice-start = ((s8[5242880]{0:T(1024)(128)(4,1)}), s8[4194304]{0:T(1024)(128)(4,1)S(1)}, s32[]{:S(2)}) async-start(s8[5242880]{0:T(1024)(128)(4,1)} %bitcast.259), calls=%async_computation | async-start | bytes 8388608
  330.1 4.6 copy-start.51
  332.9 6.2 %slice-start.1 = ((s8[5242880]{0:T(1024)(128)(4,1)}), s8[1048576]{0:T(1024)(128)(4,1)S(1)}, s32[]{:S(2)}) async-start(s8[5242880]{0:T(1024)(128)(4,1)} %bitcast.259), calls=%async_computation.1 | async-start | bytes 2097152
  332.9 6.2 %slice-start.5 = ((s8[5242880]{0:T(1024)(128)(4,1)}), s8[1048576]{0:T(1024)(128)(4,1)S(1)}, s32[]{:S(2)}) async-start(s8[5242880]{0:T(1024)(128)(4,1)} %bitcast.267), calls=%async_computation.5 | async-start | bytes 2097152
  334.7 4.4 copy-start.7
  366.8 9.2 %copy-start.32 = (bf16[4,512,6]{2,0,1:T(4,128)(2,1)S(1)}, bf16[4,512,6]{2,0,1:T(4,128)(2,1)}, u32[]{:S(2)}) copy-start(bf16[4,512,6]{2,0,1:T(4,128)(2,1)} %get-tuple-element.95) | copy-start | bytes 73732
  387.2 9.8 %copy-start.34 = (bf16[4,8,48,384]{3,2,1,0:T(8,128)(2,1)S(1)}, bf16[4,8,48,384]{3,2,1,0:T(8,128)(2,1)}, u32[]{:S(2)}) copy-start(bf16[4,8,48,384]{3,2,1,0:T(8,128)(2,1)} %get-tuple-element.32) | copy-start | bytes 3538948
  403.7 4.4 copy-start.86
  415.3 11.4 %copy-start.12 = (bf16[16,2,48,384]{3,2,0,1:T(8,128)(2,1)S(1)}, bf16[16,2,48,384]{3,2,0,1:T(8,128)(2,1)}, u32[]{:S(2)}) copy-start(bf16[16,2,48,384]{3,2,0,1:T(8,128)(2,1)} %copy.357) | copy-start | bytes 3538948
  426.7 7.8 %slice-start.2 = ((s8[6291456]{0:T(1024)(128)(4,1)}), s8[4194304]{0:T(1024)(128)(4,1)S(1)}, s32[]{:S(2)}) async-start(s8[6291456]{0:T(1024)(128)(4,1)} %bitcast.264), calls=%async_computation.2 | async-start | bytes 8388608
  428.9 5.5 slice-start.3
  428.9 5.5 copy-start.26
  515.6 4.2 copy-start.68
  518.0 15.3 %copy-start.67 = (f32[5,104]{1,0:T(8,128)S(1)}, f32[5,104]{1,0:T(8,128)}, u32[]{:S(2)}) copy-start(f32[5,104]{1,0:T(8,128)} %param.27) | copy-start | bytes 6244
  518.0 15.3 %copy-start.73 = (f32[5,104]{1,0:T(8,128)S(1)}, f32[5,104]{1,0:T(8,128)}, u32[]{:S(2)}) copy-start(f32[5,104]{1,0:T(8,128)} %param.28) | copy-start | bytes 6244
  518.0 15.3 %copy-start.74 = (f32[5,104]{1,0:T(8,128)S(1)}, f32[5,104]{1,0:T(8,128)}, u32[]{:S(2)}) copy-start(f32[5,104]{1,0:T(8,128)} %param.29) | copy-start | bytes 6244
  518.0 15.9 %copy-start.82 = (f32[144]{0:T(256)S(1)}, f32[144]{0:T(256)}, u32[]{:S(2)}) copy-start(f32[144]{0:T(256)} %param.30) | copy-start | bytes 1732
  518.0 15.9 %copy-start.83 = (f32[144]{0:T(256)S(1)}, f32[144]{0:T(256)}, u32[]{:S(2)}) copy-start(f32[144]{0:T(256)} %param.31) | copy-start | bytes 1732
  518.1 15.9 %copy-start.84 = (f32[144]{0:T(256)S(1)}, f32[144]{0:T(256)}, u32[]{:S(2)}) copy-start(f32[144]{0:T(256)} %param.32) | copy-start | bytes 1732
  518.1 16.5 %copy-start.72 = (f32[3,48]{1,0:T(4,128)S(1)}, f32[3,48]{1,0:T(4,128)}, u32[]{:S(2)}) copy-start(f32[3,48]{1,0:T(4,128)} %param.33) | copy-start | bytes 1732
  518.1 16.5 %copy-start.79 = (f32[3,48]{1,0:T(4,128)S(1)}, f32[3,48]{1,0:T(4,128)}, u32[]{:S(2)}) copy-start(f32[3,48]{1,0:T(4,128)} %param.34) | copy-start | bytes 1732
  518.1 16.5 %copy-start.80 = (f32[3,48]{1,0:T(4,128)S(1)}, f32[3,48]{1,0:T(4,128)}, u32[]{:S(2)}) copy-start(f32[3,48]{1,0:T(4,128)} %param.35) | copy-start | bytes 1732
  534.6 4.5 copy-start.47
  535.2 16.5 %copy-start.76 = (pred[8]{0:T(512)(128)(4,1)S(1)}, pred[8]{0:T(512)(128)(4,1)}, u32[]{:S(2)}) copy-start(pred[8]{0:T(512)(128)(4,1)} %copy-done.75) | copy-start | bytes 28
  559.2 10.4 %copy-start.52 = (bf16[3,48,384]{2,1,0:T(8,128)(2,1)S(1)}, bf16[3,48,384]{2,1,0:T(8,128)(2,1)}, u32[]{:S(2)}) copy-start(bf16[3,48,384]{2,1,0:T(8,128)(2,1)} %get-tuple-element.45) | copy-start | bytes 331780
  570.4 5.0 copy-start.29
  577.7 4.9 copy-start.39
  577.7 5.1 copy-start.31
  577.7 5.1 copy-start.45
  577.7 5.1 copy-start.46
  (33 other events, 81.2 us)

commit v2 on v1

--- a/solution.py
+++ b/solution.py
@@ -904,10 +904,391 @@
 
 OWN_HEADS = HEADS // RANKS
 OWN = OWN_HEADS * HDIM
+PAIRS = OWN_HEADS // 2
 RUN = OWN // 2
 COMMON = 2 * NST + HEADS
 COMMON_PAD = 384
 GROUP = 2 * BLOCK
+MIX = OWN + 2 * NST
+LANES = 128
+
+
+def mm(left, right):
+    return lax.dot_general(left, right, (((1,), (0,)), ((), ())), preferred_element_type=jnp.float32)
+
+
+def mm_t(left, right):
+    return lax.dot_general(left, right, (((1,), (1,)), ((), ())), preferred_element_type=jnp.float32)
+
+
+def t_mm(left, right):
+    return lax.dot_general(left, right, (((0,), (0,)), ((), ())), preferred_element_type=jnp.float32)
+
+
+def mm_full(left, right):
+    return lax.dot_general(
+        left, right, (((1,), (0,)), ((), ())), precision=highest, preferred_element_type=jnp.float32
+    )
+
+
+def low16(value):
+    return value.astype(jnp.bfloat16)
+
+
+def iota(shape, axis):
+    return lax.broadcasted_iota(jnp.int32, shape, axis)
+
+
+def head_spread():
+    return (iota((LANES, OWN), 1) // HDIM == iota((LANES, OWN), 0)).astype(jnp.float32)
+
+
+def head_gather():
+    return (iota((OWN, LANES), 0) // HDIM == iota((OWN, LANES), 1)).astype(jnp.float32)
+
+
+def lower_mask():
+    return iota((BLOCK, BLOCK), 0) >= iota((BLOCK, BLOCK), 1)
+
+
+def shift_down(value, k):
+    if k == 0:
+        return value
+    rolled = pltpu.roll(value, k, 0)
+    return jnp.where(iota(value.shape, 0) >= k, rolled, 0.0)
+
+
+def shift_up(value, k):
+    if k == 0:
+        return value
+    rows = value.shape[0]
+    rolled = pltpu.roll(value, rows - k, 0)
+    return jnp.where(iota(value.shape, 0) < rows - k, rolled, 0.0)
+
+
+def sigmoid(value):
+    return 1.0 / (1.0 + jnp.exp(-value))
+
+
+def softplus(value):
+    return jnp.maximum(value, 0.0) + jnp.log1p(jnp.exp(-jnp.abs(value)))
+
+
+def preact_of(u, conv):
+    total = u * conv[KCONV - 1 : KCONV] + conv[KCONV : KCONV + 1]
+    for tap in range(KCONV - 1):
+        total = total + shift_down(u, KCONV - 1 - tap) * conv[tap : tap + 1]
+    return total
+
+
+def steps_of(raw, heads, live):
+    step = softplus(raw + heads[0:1]) * live * heads[3:4]
+    return (step, -jnp.exp(heads[1:2]) * step)
+
+
+def decay_of(cumul, cumul_t, h):
+    return jnp.exp(jnp.minimum(cumul[:, h : h + 1] - cumul_t[h : h + 1, :], 0.0))
+
+
+def lane_half(value, side):
+    lanes = iota(value.shape, 1)
+    return jnp.where((lanes >= HDIM) == (side == 1), value, jnp.zeros_like(value))
+
+
+def block_parts(step, logdec, spread):
+    cumul = mm_full(lower_mask().astype(jnp.float32), logdec)
+    return (cumul, jnp.transpose(cumul), mm_full(step, spread), mm_full(cumul, spread))
+
+
+def forward_group(live, tok, cot, w_own, w_com, w_out, gain_in, gain_out, conv, heads, skip, select):
+    token_rows = tok[...].astype(jnp.float32)
+    scaling = lax.rsqrt(jnp.mean(token_rows * token_rows, axis=1, keepdims=True) + norm_eps)
+    normed = low16(token_rows * scaling * gain_in[...])
+    gate_part = mm(normed, w_own[:, :OWN])
+    conv_in = jnp.concatenate([mm(normed, w_own[:, OWN:]), mm(normed, w_com[:, : 2 * NST])], axis=1)
+    raw = mm_full(mm(normed, w_com[:, 2 * NST :]), select[...])
+    preact = preact_of(conv_in, conv[...])
+    act = low16(preact * sigmoid(preact))
+    step, logdec = steps_of(raw, heads[...], live)
+    spread = head_spread()
+    lower = lower_mask()
+    outs = []
+    state = None
+    for k in range(2):
+        rows = slice(k * BLOCK, (k + 1) * BLOCK)
+        values, keys, queries = (act[rows, :OWN], act[rows, OWN : OWN + NST], act[rows, OWN + NST :])
+        cumul, cumul_t, step_w, cumul_w = block_parts(step[rows], logdec[rows], spread)
+        gram = jnp.where(lower, mm_t(queries, keys), 0.0)
+        values_f = values.astype(jnp.float32)
+        stepped = low16(values_f * step_w)
+        pieces = []
+        for pair in range(PAIRS):
+            lanes = slice(pair * LANES, (pair + 1) * LANES)
+            piece = 0.0
+            for side in range(2):
+                mixing = low16(gram * decay_of(cumul, cumul_t, 2 * pair + side))
+                piece = piece + mm(mixing, lane_half(stepped[:, lanes], side))
+            pieces.append(piece)
+        out = jnp.concatenate(pieces, axis=1) + skip[...] * values_f
+        if state is not None:
+            out = out + jnp.exp(cumul_w) * mm(queries, state)
+        else:
+            weighting = jnp.exp(cumul_w[BLOCK - 1 :] - cumul_w) * step_w
+            state = low16(t_mm(keys, low16(weighting * values_f)))
+        outs.append(out)
+    mixed = jnp.concatenate(outs, axis=0)
+    grad = jnp.where(live > 0.0, cot[...], jnp.zeros_like(cot[...]))
+    grad_normed_out = mm_t(grad, w_out[...])
+    gated = mixed * gate_part * sigmoid(gate_part)
+    stats = (
+        jnp.sum(gated * gated, axis=1, keepdims=True),
+        jnp.sum(grad_normed_out * gain_out[...] * gated, axis=1, keepdims=True),
+    )
+    return (normed, gate_part, conv_in, raw, act, mixed, grad_normed_out, stats)
+
+
+def live_of(lens, g):
+    rows = iota((GROUP, 1), 0).astype(jnp.float32)
+    chosen = jnp.sum(jnp.where(iota(lens.shape, 0) == g, lens, 0.0), axis=0, keepdims=True)[:, :1]
+    return (rows < chosen).astype(jnp.float32)
+
+
+def forward_kernel(
+    lens, tok, cot, w_own, w_com, w_out, gain_in, gain_out, conv, heads, skip, select,
+    normed, gate_part, conv_in, raw, act, mixed, grad_normed_out, stats
+):
+    g = pl.program_id(0)
+    live = live_of(lens[...], g)
+    results = forward_group(
+        live, tok, cot, w_own, w_com, w_out, gain_in, gain_out, conv, heads, skip, select
+    )
+    for ref, value in zip((normed, gate_part, conv_in, raw, act, mixed, grad_normed_out), results):
+        ref[...] = value
+    lanes = iota((GROUP, LANES), 1)
+    columns = jnp.where(lanes == 2 * g, results[7][0], 0.0) + jnp.where(lanes == 2 * g + 1, results[7][1], 0.0)
+
+    @pl.when(g == 0)
+    def first():
+        stats[...] = jnp.zeros_like(stats)
+
+    stats[...] += jnp.transpose(columns)[:8]
+
+
+def full_spec(shape):
+    return pl.BlockSpec(shape, lambda g: (0,) * len(shape))
+
+
+def group_spec(width):
+    return pl.BlockSpec((GROUP, width), lambda g: (g, 0))
+
+
+VMEM_GRANT = 60 * 1024 * 1024
+
+
+def run_forward(lens, tok, cot, w_own, w_com, w_out, gain_in, gain_out, conv, heads, skip, select):
+    f32, bf16 = (jnp.float32, jnp.bfloat16)
+    rows = QUADS * GROUP
+    widths = ((D, bf16), (OWN, f32), (MIX, f32), (LANES, f32), (MIX, bf16), (OWN, f32), (OWN, f32))
+    return pl.pallas_call(
+        forward_kernel,
+        grid=(QUADS,),
+        in_specs=[full_spec(lens.shape), group_spec(D), group_spec(D)]
+        + [full_spec(a.shape) for a in (w_own, w_com, w_out, gain_in, gain_out, conv, heads, skip, select)],
+        out_specs=[group_spec(w) for w, kind in widths] + [full_spec((8, GROUP))],
+        out_shape=[jax.ShapeDtypeStruct((rows, w), kind) for w, kind in widths]
+        + [jax.ShapeDtypeStruct((8, GROUP), f32)],
+        compiler_params=pltpu.CompilerParams(vmem_limit_bytes=VMEM_GRANT),
+    )(lens, tok, cot, w_own, w_com, w_out, gain_in, gain_out, conv, heads, skip, select)
+
+
+def backward_block(k, act, dmix, step, logdec, skip, state, state_grad, spread, gather):
+    values, keys, queries = (act[:, :OWN], act[:, OWN : OWN + NST], act[:, OWN + NST :])
+    lower = lower_mask()
+    cumul, cumul_t, step_w, cumul_w = block_parts(step, logdec, spread)
+    step_t = jnp.transpose(step)
+    gram = jnp.where(lower, mm_t(queries, keys), 0.0)
+    values_f = values.astype(jnp.float32)
+    dmix_f = dmix.astype(jnp.float32)
+    lanes_h = iota((BLOCK, LANES), 1)
+    rows_h = iota((8, BLOCK), 0)
+    grad_gram = 0.0
+    row_sums = jnp.zeros((BLOCK, LANES), jnp.float32)
+    col_sums = jnp.zeros((8, BLOCK), jnp.float32)
+    pieces = []
+    for pair in range(PAIRS):
+        lanes = slice(pair * LANES, (pair + 1) * LANES)
+        piece = 0.0
+        for side in range(2):
+            h = 2 * pair + side
+            decay = decay_of(cumul, cumul_t, h)
+            dm_half = lane_half(dmix[:, lanes], side)
+            grad_mixing = mm_t(dm_half, values[:, lanes])
+            step_row = step_t[h : h + 1, :]
+            grad_gram = grad_gram + grad_mixing * decay * step_row
+            mixing = gram * decay
+            piece = piece + t_mm(low16(mixing), dm_half)
+            product = grad_mixing * mixing
+            col_sums = jnp.where(rows_h == h, jnp.sum(product, axis=0, keepdims=True), col_sums)
+            row_sums = jnp.where(
+                lanes_h == h, jnp.sum(product * step_row, axis=1, keepdims=True), row_sums
+            )
+        pieces.append(piece)
+    grad_values = jnp.concatenate(pieces, axis=1) * step_w + skip * dmix_f
+    grad_skip = jnp.sum(dmix_f * values_f, axis=0, keepdims=True)
+    grad_gram = low16(jnp.where(lower, grad_gram, 0.0))
+    grad_queries = mm(grad_gram, keys)
+    grad_keys = t_mm(grad_gram, queries)
+    columns = jnp.transpose(jnp.concatenate([col_sums, jnp.zeros((LANES - 8, BLOCK), jnp.float32)], axis=0))
+    grad_step = columns
+    grad_cumul = row_sums - columns * step
+    if k == 1:
+        entering = jnp.exp(cumul_w) * dmix_f
+        entering_low = low16(entering)
+        crossed = mm(queries, state)
+        grad_cumul = grad_cumul + mm_full(entering * crossed, gather)
+        grad_queries = grad_queries + mm_t(entering_low, state)
+        before = low16(t_mm(queries, entering_low))
+    else:
+        tail = jnp.exp(cumul_w[BLOCK - 1 :] - cumul_w)
+        weighting = tail * step_w
+        back = mm(keys, state_grad)
+        grad_values = grad_values + weighting * back
+        grad_keys = grad_keys + mm_t(low16(weighting * values_f), state_grad)
+        grad_weight = mm_full(values_f * back, gather)
+        tail_h = jnp.exp(cumul[BLOCK - 1 :] - cumul)
+        grad_step = grad_step + grad_weight * tail_h
+        part = grad_weight * tail_h * step
+        last = iota((BLOCK, LANES), 0) == BLOCK - 1
+        grad_cumul = grad_cumul - part + jnp.where(last, jnp.sum(part, axis=0, keepdims=True), 0.0)
+        before = None
+    upper = (iota((BLOCK, BLOCK), 0) <= iota((BLOCK, BLOCK), 1)).astype(jnp.float32)
+    grad_logdec = mm_full(upper, grad_cumul)
+    return (grad_values, grad_keys, grad_queries, grad_step, grad_logdec, grad_skip, before)
+
+
+def backward_kernel(
+    lens, stats, cot, normed, gate_part, conv_in, raw, act, mixed, grad_normed_out,
+    w_own, w_com, w_out, gain_out, conv, heads, skip, select,
+    branch, grad_normed, g_out, g_own, g_com, small_conv, small_head, small_wide,
+    acc_out, acc_in
+):
+    g = pl.program_id(0)
+    live = live_of(lens[...], g)
+
+    @pl.when(g == 0)
+    def first():
+        acc_out[...] = jnp.zeros_like(acc_out)
+        acc_in[...] = jnp.zeros_like(acc_in)
+        small_conv[...] = jnp.zeros_like(small_conv)
+        small_head[...] = jnp.zeros_like(small_head)
+        small_wide[...] = jnp.zeros_like(small_wide)
+
+    padded = jnp.concatenate([stats[...], jnp.zeros((LANES - 8, GROUP), jnp.float32)], axis=0)
+    columns = jnp.transpose(padded)
+    lanes = iota((GROUP, LANES), 1)
+    power = jnp.sum(jnp.where(lanes == 2 * g, columns, 0.0), axis=1, keepdims=True)
+    along = jnp.sum(jnp.where(lanes == 2 * g + 1, columns, 0.0), axis=1, keepdims=True)
+    scale_out = lax.rsqrt(power * (1.0 / DIN) + norm_eps)
+    gate_v, mixed_v, gno = (gate_part[...], mixed[...], grad_normed_out[...])
+    sig = sigmoid(gate_v)
+    gate_act = gate_v * sig
+    gated = mixed_v * gate_act
+    normed_out = low16(gated * scale_out * gain_out[...])
+    branch[...] = low16(mm(normed_out, w_out[...]))
+    grad = jnp.where(live > 0.0, cot[...], jnp.zeros_like(cot[...]))
+    acc_out[...] += t_mm(normed_out, grad)
+    scaled = gno * scale_out
+    grad_gated = scaled * gain_out[...] - gated * (scale_out * scale_out * scale_out * along * (1.0 / DIN))
+    gain_sum = jnp.sum(scaled * gated, axis=0, keepdims=True)
+    grad_gate = grad_gated * mixed_v * (sig * (1.0 + gate_v * (1.0 - sig)))
+    dmix = low16(grad_gated * gate_act)
+
+    act_v = act[...]
+    raw_v = raw[...]
+    heads_v = heads[...]
+    step, logdec = steps_of(raw_v, heads_v, live)
+    spread, gather = (head_spread(), head_gather())
+    rows0, rows1 = (slice(0, BLOCK), slice(BLOCK, GROUP))
+    cumul0 = mm_full(lower_mask().astype(jnp.float32), logdec[rows0])
+    cumul0_w = mm_full(cumul0, spread)
+    weighting = jnp.exp(cumul0_w[BLOCK - 1 :] - cumul0_w) * mm_full(step[rows0], spread)
+    state = low16(
+        t_mm(act_v[rows0, OWN : OWN + NST], low16(weighting * act_v[rows0, :OWN].astype(jnp.float32)))
+    )
+    late = backward_block(
+        1, act_v[rows1], dmix[rows1], step[rows1], logdec[rows1], skip[...], state, None, spread, gather
+    )
+    early = backward_block(
+        0, act_v[rows0], dmix[rows0], step[rows0], logdec[rows0], skip[...], None, late[6], spread, gather
+    )
+    grad_act = jnp.concatenate([jnp.concatenate(part[:3], axis=1) for part in (early, late)], axis=0)
+    grad_step = jnp.concatenate([early[3], late[3]], axis=0)
+    grad_logdec = jnp.concatenate([early[4], late[4]], axis=0)
+    rate = jnp.exp(heads_v[1:2])
+    grad_raw = (grad_step - rate * grad_logdec) * live * heads_v[3:4] * sigmoid(raw_v + heads_v[0:1])
+    u = conv_in[...]
+    conv_v = conv[...]
+    preact = preact_of(u, conv_v)
+    sig_q = sigmoid(preact)
+    grad_pre = grad_act * (sig_q * (1.0 + preact * (1.0 - sig_q)))
+    grad_u = grad_pre * conv_v[KCONV - 1 : KCONV]
+    taps = []
+    for tap in range(KCONV):
+        lag = KCONV - 1 - tap
+        if lag:
+            grad_u = grad_u + shift_up(grad_pre, lag) * conv_v[tap : tap + 1]
+        taps.append(jnp.sum(grad_pre * shift_down(u, lag), axis=0, keepdims=True))
+    taps.append(jnp.sum(grad_pre, axis=0, keepdims=True))
+    small_conv[...] += jnp.concatenate(taps + [jnp.zeros((3, MIX), jnp.float32)], axis=0)
+    small_head[...] += jnp.concatenate(
+        [
+            jnp.sum(grad_raw, axis=0, keepdims=True),
+            jnp.sum(grad_logdec * logdec, axis=0, keepdims=True),
+            jnp.zeros((6, LANES), jnp.float32),
+        ],
+        axis=0,
+    )
+    small_wide[...] += jnp.concatenate(
+        [gain_sum, early[5] + late[5], jnp.zeros((6, OWN), jnp.float32)], axis=0
+    )
+    raw_wide = mm_t(low16(grad_raw), low16(select[...]))
+    grad_proj = low16(jnp.concatenate([grad_gate, grad_u, raw_wide], axis=1))
+    grad_normed[...] = low16(
+        mm_t(grad_proj[:, : 2 * OWN], w_own[...]) + mm_t(grad_proj[:, 2 * OWN :], w_com[...])
+    )
+    acc_in[...] += t_mm(normed[...], grad_proj)
+
+    @pl.when(g == QUADS - 1)
+    def last():
+        g_out[...] = low16(acc_out[...])
+        g_own[...] = low16(acc_in[:, : 2 * OWN])
+        g_com[...] = low16(acc_in[:, 2 * OWN :])
+
+
+def run_backward(
+    lens, stats, cot, normed, gate_part, conv_in, raw, act, mixed, grad_normed_out,
+    w_own, w_com, w_out, gain_out, conv, heads, skip, select
+):
+    f32, bf16 = (jnp.float32, jnp.bfloat16)
+    rows = QUADS * GROUP
+    fixed = (w_own, w_com, w_out, gain_out, conv, heads, skip, select)
+    grouped = (cot, normed, gate_part, conv_in, raw, act, mixed, grad_normed_out)
+    ends = (
+        ((OWN, D), bf16), ((D, 2 * OWN), bf16), ((D, COMMON_PAD), bf16),
+        ((8, MIX), f32), ((8, LANES), f32), ((8, OWN), f32),
+    )
+    return pl.pallas_call(
+        backward_kernel,
+        grid=(QUADS,),
+        in_specs=[full_spec(lens.shape), full_spec(stats.shape)]
+        + [group_spec(a.shape[1]) for a in grouped]
+        + [full_spec(a.shape) for a in fixed],
+        out_specs=[group_spec(D), group_spec(D)] + [full_spec(s) for s, kind in ends],
+        out_shape=[jax.ShapeDtypeStruct((rows, D), bf16)] * 2
+        + [jax.ShapeDtypeStruct(s, kind) for s, kind in ends],
+        scratch_shapes=[pltpu.VMEM((OWN, D), f32), pltpu.VMEM((D, 2 * OWN + COMMON_PAD), f32)],
+        compiler_params=pltpu.CompilerParams(vmem_limit_bytes=VMEM_GRANT),
+    )(lens, stats, *grouped, *fixed)
 
 
 def pick_runs(array, plane_runs, quad, core):
@@ -943,29 +1324,6 @@
     rows = array.shape[1]
     split = array.reshape(QUADS, 2, rows, 2, RUN)
     return split.transpose(2, 1, 3, 0, 4).reshape(rows, DIN)
-
-
-def mixer_quad(extended, step_raw, conv_par, head_values, live_rows):
-    rows = step_raw.shape[1]
-    preact = conv_par[KCONV][None, None, :]
-    for tap in range(KCONV):
-        preact = preact + conv_par[tap][None, None, :] * extended[:, tap : tap + rows]
-    conv_act = jax.nn.silu(preact)
-    step_size = jax.nn.softplus(step_raw + head_values[0]) * live_rows[:, :, None]
-    logdec = -jnp.exp(head_values[1]) * step_size
-    return (conv_act, step_size, logdec)
-
-
-def two_blocks(values, keys_in, queries, step_size, logdec, skip_gain):
-    start = jnp.zeros((OWN_HEADS, HDIM, NST), jnp.float32)
-    outs = []
-    for k in range(2):
-        rows = slice(k * BLOCK, (k + 1) * BLOCK)
-        out, start = block_full(
-            values[rows], keys_in[rows], queries[rows], step_size[rows], logdec[rows], skip_gain, start
-        )
-        outs.append(out)
-    return jnp.concatenate(outs, axis=0)
 
 
 def per_device_quad(
@@ -1013,62 +1371,35 @@
         .reshape(PLANES * RANKS, 5, 104).transpose(1, 0, 2).reshape(5, CONVC)
     )
     lens = lax.dynamic_index_in_dim(extras, plane, 0, False)[::2, 0, 14] + BLOCK
-    w_com = w_com.reshape(D, COMMON_PAD)[:, :COMMON]
+    w_com = w_com.reshape(D, COMMON_PAD)
     live = (jnp.arange(GROUP)[None, :] < lens[:, None]).astype(f32)
+    lens_rows = jnp.pad(jnp.broadcast_to(lens[:, None], (QUADS, LANES)), ((0, 8 - QUADS), (0, 0)))
     conv_own = jnp.concatenate([pick_runs(conv_par[:, :DIN], 2, quad, core), conv_par[:, DIN:]], axis=1)
-    gain_out = pick_runs(gain_par[D:], 2, quad, core)
+    conv_own = jnp.pad(conv_own, ((0, 3), (0, 0)))
+    gain_out = pick_runs(gain_par[D:], 2, quad, core)[None, :]
     head_own = pick_runs(head_params, 2, quad, core)
-
-    scaling = lax.rsqrt(jnp.mean(jnp.square(tok.astype(f32)), axis=1, keepdims=True) + norm_eps)
-    normed = (tok.astype(f32) * scaling * gain_par[:D]).astype(bf16)
-    proj_own = jnp.dot(normed, w_own, preferred_element_type=f32)
-    proj_com = jnp.dot(normed, w_com, preferred_element_type=f32)
-    gate_part = proj_own[:, :OWN]
-    conv_in = jnp.concatenate([proj_own[:, OWN:], proj_com[:, : 2 * NST]], axis=1)
-    step_raw = pick_runs(proj_com[:, 2 * NST :], 2, quad, core)
-    extended = jnp.pad(conv_in.reshape(QUADS, GROUP, -1), ((0, 0), (KCONV - 1, 0), (0, 0)))
-    (conv_act, step_size, logdec), pull_mixer = jax.vjp(
-        lambda *a: mixer_quad(*a, live), extended, step_raw.reshape(QUADS, GROUP, OWN_HEADS), conv_own, head_own
-    )
-    used = as_float(conv_act.astype(bf16))
-    values = used[:, :, :OWN].reshape(QUADS, GROUP, OWN_HEADS, HDIM)
-    keys_in = used[:, :, OWN : OWN + NST]
-    queries = used[:, :, OWN + NST :]
-    mixed, pull_ssd = jax.vjp(
-        jax.vmap(two_blocks, in_axes=(0, 0, 0, 0, 0, None)), values, keys_in, queries, step_size, logdec, head_own[2]
-    )
-    mixed = mixed.reshape(RANKS * BLOCK, OWN)
-    out_grad = (cot.astype(f32) * live.reshape(-1, 1)).astype(bf16)
-    grad_normed_out = contract_cols(out_grad, w_out)
-    sig = jax.nn.sigmoid(gate_part)
-    gate_act = gate_part * sig
-    gated = mixed * gate_act
-    weighted = grad_normed_out * gain_out
-    stats = jnp.stack([jnp.sum(gated * gated, axis=1), jnp.sum(weighted * gated, axis=1)])
-    stats = stats.reshape(32, 128)
+    heads = jnp.pad(
+        jnp.concatenate([head_own, jnp.ones((1, OWN_HEADS), f32)]), ((0, 4), (0, LANES - OWN_HEADS))
+    )
+    skip = jnp.repeat(head_own[2], HDIM)[None, :]
+    head_index = pick_runs(jnp.arange(HEADS)[None, :], 2, quad, core)[0]
+    select = (iota((LANES, OWN_HEADS), 0) == head_index[None, :]).astype(f32)
+    select = jnp.pad(select, ((0, 0), (0, LANES - OWN_HEADS)))
+
+    normed, gate_part, conv_in, raw, act, mixed, grad_normed_out, stats = run_forward(
+        lens_rows, tok, cot, w_own, w_com, w_out, gain_par[None, :D], gain_out, conv_own, heads, skip, select
+    )
     shared = share(1, stats)
     ranks = lax.broadcasted_iota(jnp.int32, (RANKS, 1, 1), 0)
-    total = jnp.sum(jnp.where(ranks == rank, stats[None], shared), axis=0).reshape(2, RANKS * BLOCK, 1)
-    scale_out = lax.rsqrt(total[0] / DIN + norm_eps)
-    normed_out = (gated * scale_out * gain_out).astype(bf16)
-    branch = jnp.dot(normed_out, w_out, preferred_element_type=f32).astype(bf16)
-    grad_out_w = contract_rows(normed_out, out_grad).astype(bf16)
-    grad_gated = scale_out * weighted - gated * (scale_out**3 * total[1] / DIN)
-    grad_gain_out = jnp.sum(grad_normed_out * gated * scale_out, axis=0)
-    grad_gate = grad_gated * mixed * (sig * (1.0 + gate_part * (1.0 - sig)))
-    mixed_back = as_float((grad_gated * gate_act).astype(bf16))
-    grad_values, grad_keys, grad_queries, grad_step, grad_logdec, grad_skip = pull_ssd(
-        mixed_back.reshape(QUADS, GROUP, OWN_HEADS, HDIM)
-    )
-    grad_act = jnp.concatenate([grad_values.reshape(QUADS, GROUP, OWN), grad_keys, grad_queries], axis=2)
-    grad_ext, grad_raw, grad_conv_own, grad_head_own = pull_mixer((grad_act, grad_step, grad_logdec))
-    grad_conv_in = grad_ext[:, KCONV - 1 :].reshape(RANKS * BLOCK, OWN + 2 * NST)
-    grad_proj_own = jnp.concatenate([grad_gate, grad_conv_in[:, :OWN]], axis=1).astype(bf16)
-    grad_raw = put_runs(grad_raw.reshape(RANKS * BLOCK, OWN_HEADS), quad, core)
-    grad_proj_com = jnp.concatenate([grad_conv_in[:, OWN:], grad_raw], axis=1).astype(bf16)
-    grad_normed = (contract_cols(grad_proj_own, w_own) + contract_cols(grad_proj_com, w_com)).astype(bf16)
-    grad_own_w = contract_rows(normed, grad_proj_own).astype(bf16)
-    grad_com_w = jnp.pad(contract_rows(normed, grad_proj_com), ((0, 0), (0, COMMON_PAD - COMMON))).astype(bf16)
+    total = jnp.sum(jnp.where(ranks == rank, stats[None], shared), axis=0)
+    branch, grad_normed, grad_out_w, grad_own_w, grad_com_w, small_conv, small_head, small_wide = run_backward(
+        lens_rows, total, cot, normed, gate_part, conv_in, raw, act, mixed, grad_normed_out,
+        w_own, w_com, w_out, gain_out, conv_own, heads, skip, select
+    )
+    grad_conv_own = small_conv[: KCONV + 1]
+    grad_gain_out = small_wide[0]
+    grad_skip = jnp.sum(small_wide[1].reshape(OWN_HEADS, HDIM), axis=1)
+    grad_head_own = jnp.concatenate([small_head[:2, :OWN_HEADS], grad_skip[None, :]])
 
     def by_core(array, lead):
         split = array.reshape((lead, 2) + array.shape[1:]) if array.shape[0] == 2 * lead else array
@@ -1122,7 +1453,6 @@
     grad_conv = jnp.concatenate(
         [put_runs(grad_conv_own[:, :OWN], quad, core), grad_conv_own[:, OWN:]], axis=1
     ).reshape(5, 32, 104).transpose(1, 0, 2).reshape(32, 520)
-    grad_head_own = grad_head_own + jnp.stack([jnp.zeros_like(grad_skip), jnp.zeros_like(grad_skip), grad_skip])
     grad_head = jnp.broadcast_to(put_runs(grad_head_own, quad, core).reshape(1, 144), (32, 144))
     small = jnp.concatenate([grad_gains, grad_conv, grad_head, jnp.zeros((32, 216), f32)], axis=1)
     small = small.reshape(32, 8, 128)

time: 591 us -> 419 us (0.71)
  matrix products: 133 us -> 0 us
  Pallas kernels: 222 us -> 323 us
  other arithmetic: 135 us -> 45.6 us
  local copies, waits for them, and re-layouts: 92.5 us -> 42.8 us
    dot_general x34 -> x0, matrix products: 133 us -> none  [the longest x6 34 us: block_out(): intra_part = jnp.einsum('htu,uhp->thp', mixing, values, precision=highest)]
    pallas_call x0 -> x2, Pallas kernels: none -> 102 us  [the longest x1 66 us: run_backward(): pl.pallas_call(backward_kernel, grid=(QUADS,), in_specs=[full_spec(lens.s...]
    convert_element_type x3 -> x0, other arithmetic: 29.6 us -> none  [the longest x2 17.1 us: per_device_quad(): out_grad = (cot.astype(f32) * live.reshape(-1, 1)).astype(bf16)]
    reduce_sum x5 -> x2, other arithmetic: 20.3 us -> 1.72 us  [the longest x1 1.6 us: per_device_quad(): total = jnp.sum(jnp.where(ranks == rank, stats[None], shared), axis=0)]
    unnamed x200 -> x54, local copies, waits for them, and re-layouts: 19 us -> 3.02 us
    another operation x4 -> x2, other arithmetic: 14.6 us -> 0.01 us  [the longest x1 0.01 us: pick_runs(): split = array.reshape(lead + (2, 2, QUADS, width))]
    reshape x3 -> x0, local copies, waits for them, and re-layouts: 14.1 us -> none  [the longest x1 6.13 us: per_device_quad(): conv_in.reshape(QUADS, GROUP, -1)]
    mul x4 -> x0, other arithmetic: 12.6 us -> none  [the longest x1 9.9 us: mixer_quad(): preact = preact + conv_par[tap][None, None, :] * extended[:, tap:tap + rows]]
where the time goes in v2:
time: 419 us; the launch traced here: 413 us
  Pallas kernels  323 us (77%)
  other arithmetic  45.6 us (11%)
  local copies, waits for them, and re-layouts  42.8 us (10%)
    pallas_call x1, Pallas kernels, gather_all(): pl.pallas_call(gather_kernel, out_shape=[jax.ShapeDtypeStruct(s, bf16) fo...  105 us
    pallas_call x2, Pallas kernels, push(): pl.pallas_call(functools.partial(push_kernel, len(quads), len(planes), le...  89.3 us
    pallas_call x1, Pallas kernels, run_backward(): pl.pallas_call(backward_kernel, grid=(QUADS,), in_specs=[full_spec(lens.s...  66 us
    pallas_call x1, Pallas kernels, run_forward(): pl.pallas_call(forward_kernel, grid=(QUADS,), in_specs=[full_spec(lens.sh...  35.6 us
    pallas_call x1, Pallas kernels, core_swap(): pl.pallas_call(core_kernel, out_shape=[jax.ShapeDtypeStruct(a.shape[1:],...  11.4 us
    convert_element_type x2, other arithmetic, per_device_quad(): (own_part(a, core).astype(f32) + b.astype(f32)).astype(bf16)  10.5 us
    another operation x3, local copies, waits for them, and re-layouts, by_core(): array.reshape((lead, 2) + array.shape[1:])  10.5 us
    pallas_call x1, Pallas kernels, to_owners(): pl.pallas_call(owners_kernel, out_shape=jax.ShapeDtypeStruct(array.shape,...  10.1 us

profile of v2, /device:TPU:0, one launch (start us, length us, event | category | flops | bytes accessed | tf_op | source)
XLA Modules:
  0.0 413.5 jit_solution(8091401487284188741)
XLA Ops:
  0.7 1.4 convert_element_type.148
  2.1 0.5 reshape.269
  2.6 0.3 copy.60
  3.2 0.5 reshape.271
  3.7 0.3 copy.61
  4.2 0.9 pad_maximum_fusion.1.wz
  5.7 0.6 pad.31.wc
  6.3 0.7 convert_element_type.152.wo
  7.1 105.2 %shard_map.305 = (bf16[8,256,1536]{2,1,0:T(8,128)(2,1)}, bf16[8,256,1536]{2,1,0:T(8,128)(2,1)}, bf16[4,8,48,768]{3,2,1,0:T(8,128)(2,1)}, bf16[4,8,48,384]{3,2,1,...) custom-call(bf16[256,1536]{1,0:T(8,128)(2,1)} %tok.1, bf16[256,1536]{1,0:T(8,128)(2,1)} %cot.1, ...), custom_call_target="tpu_custom_call" | custom-call | tf_op jit(solution)/shard_map/pallas_call | solution.py:674
  112.3 1.2 slice_convert_fusion
  113.5 0.3 slice.115
  113.8 0.3 reshape.282
  114.6 0.6 select_maximum_fusion.conv
  115.2 0.4 slice.91
  115.7 0.6 broadcast_in_dim_reshape.6.gain_out
  116.5 0.7 pad.33.lens
  117.3 0.6 pad_convert_fusion.select
  118.1 0.6 select_select_fusion.heads
  118.9 0.6 broadcast_in_dim_reshape.7.skip
  119.6 0.5 reshape.281
  120.0 0.6 broadcast_in_dim.75.gain_in
  120.6 35.6 %shard_map.306 = (bf16[2048,1536]{1,0:T(8,128)(2,1)}, f32[2048,384]{1,0:T(8,128)}, f32[2048,640]{1,0:T(8,128)}, f32[2048,128]{1,0:T(8,128)}, bf16[2048,640]{1,0:...) custom-call(f32[8,128]{1,0:T(8,128)} %pad.33.lens, bf16[2048,1536]{1,0:T(8,128)(2,1)} %bitcast.90, ...), custom_call_target="tpu_custom_call" | custom-call | tf_op jit(solution)/shard_map/pallas_call | solution.py:1092
  156.2 5.7 %shard_map.307 = f32[8,8,512]{2,1,0:T(8,128)} custom-call(f32[8,512]{1,0:T(8,128)} %get-tuple-element.53.source), custom_call_target="tpu_custom_call" | custom-call | tf_op jit(solution)/shard_map/pallas_call | solution.py:895
  161.9 1.6 select_reduce_fusion.1.stats
  163.5 66.0 %shard_map.308 = (bf16[2048,1536]{1,0:T(8,128)(2,1)}, bf16[2048,1536]{1,0:T(8,128)(2,1)}, bf16[384,1536]{1,0:T(8,128)(2,1)}, bf16[1536,768]{1,0:T(8,128)(2,1)}, ...) custom-call(f32[8,128]{1,0:T(8,128)} %pad.33.lens, ...), custom_call_target="tpu_custom_call" | custom-call | tf_op jit(solution)/shard_map/pallas_call | solution.py:1280
  229.6 0.8 slice_reduce_fusion
  230.7 0.7 slice.104
  231.7 6.0 %copy.87 = bf16[4,2,256,1536]{3,2,0,1:T(8,128)(2,1)} copy(bf16[4,2,256,1536]{3,2,1,0:T(8,128)(2,1)} %bitcast.94) | data formatting | bytes 12582912 | tf_op jit(solution)/shard_map/reshape;reshape | solution.py:1405
  237.7 3.3 copy.88
  241.1 1.1 copy.89
  242.2 11.4 %shard_map.309 = (bf16[4,256,1536]{2,1,0:T(8,128)(2,1)}, bf16[4,256,1536]{2,1,0:T(8,128)(2,1)}, bf16[16,48,384]{2,1,0:T(8,128)(2,1)}) custom-call(bf16[2,4,256,1536]{3,2,1,0:T(8,128)(2,1)} %bitcast.80, bf16[2,4,256,1536]{3,2,1,0:T(8,128)(2,1)} %bitcast.79, bf16[2,16,48,384]{3,2,1,0:T(8,128)(2,1)} %bitcast.87), custom_call_target="tpu_custom_call" | custom-call | tf_op jit(solution)/shard_map/pallas_call | solution.py:705
  253.6 1.2 fusion.11
  254.8 0.9 copy.90
  255.7 9.3 %fusion = (bf16[4,256,1536]{2,1,0:T(8,128)(2,1)}, bf16[4,256,1536]{2,1,0:T(8,128)(2,1)}) fusion(bf16[4,256,1536]{2,1,0:T(8,128)(2,1)} %get-tuple-element.65, bf16[4,2,256,1536]{3,2,0,1:T(8,128)(2,1)} %copy.87, s32[]{:T(128)S(6)} %select_n.68, bf16[4,256,1536]{2,1,0:T(8,128)(2,1)} %get-tuple-element.64, bf16[4,2,256,1536]{3,2,0,1:T(8,128)(2,1)} %copy.88), kind=kLoop, calls=%fused_computation.1 | loop fusion | flops 12582912 | bytes 18874372 | tf_op jit(solution)/shard_map/convert_element_type | solution.py:1419
  265.0 78.5 %shard_map.310 = (bf16[3,256,1536]{2,1,0:T(8,128)(2,1)}, bf16[3,256,1536]{2,1,0:T(8,128)(2,1)}, bf16[3,4,48,384]{3,2,1,0:T(8,128)(2,1)}, bf16[3,8,48,768]{3,2,1,0:T(8,128)(2,1)}, bf16[4,96,1536]{2,1,0:T(8,128)(2,1)}) custom-call(bf16[4,256,1536]{2,1,0:T(8,128)(2,1)} %get-tuple-element.114.refs_0_, bf16[4,256,1536]{2,1,0:T(8,128)(2,1)} %get-tuple-element.113.refs_1_, ...), custom_call_target="tpu_custom_call" | custom-call | tf_op jit(solution)/shard_map/pallas_call | solution.py:831
  343.5 2.4 convert_reduce_fusion
  345.9 0.2 fusion.4
  346.3 0.7 fusion.7
  348.2 0.7 copy.78
  348.9 10.1 %shard_map.312 = f32[32,8,128]{2,1,0:T(8,128)} custom-call(f32[32,8,128]{2,1,0:T(8,128)} %bitcast.107), custom_call_target="tpu_custom_call" | custom-call | tf_op jit(solution)/shard_map/pallas_call | solution.py:868
  359.0 1.1 select_reduce_fusion
  360.2 0.6 multiply_subtract_fusion.2
  360.9 0.6 multiply_subtract_fusion.4
  361.5 0.6 multiply_subtract_fusion.3
  362.2 1.9 convert_reduce_fusion.2
  364.0 2.1 fusion.10.refs_1_
  366.2 1.6 fusion.13.refs_0_
  367.8 10.8 %shard_map.311 = (bf16[3,48,384]{2,1,0:T(8,128)(2,1)}, bf16[8,48,768]{2,1,0:T(8,128)(2,1)}) custom-call(bf16[4,48,384]{2,1,0:T(8,128)(2,1)} %fusion.13.refs_0_, bf16[8,48,768]{2,1,0:T(8,128)(2,1)} %fusion.10.refs_1_), custom_call_target="tpu_custom_call" | custom-call | tf_op jit(solution)/shard_map/pallas_call | solution.py:831
  378.7 1.4 select_convert_fusion
  380.1 1.1 fusion.31
  381.1 2.5 reshape.292
  383.6 2.5 copy.71
  386.2 2.7 reshape.293
  388.8 2.5 reshape.294
  391.3 2.6 copy.72
  393.9 2.7 reshape.295
  396.6 0.8 dynamic-slice_bitcast_fusion.1
  397.4 5.0 %multiply_subtract_fusion = (f32[48,6448]{1,0:T(8,128)}, f32[48,6448]{1,0:T(8,128)}, f32[48,6448]{1,0:T(8,128)}) fusion(f32[48,6448]{1,0:T(8,128)} %param.21, f32[48,304]{1,0:T(8,128)S(1)} %slice_add_fusion, f32[48,3072]{1,0:T(8,128)} %reshape.295, f32[48,3072]{1,0:T(8,128)} %reshape.293, f32[48,6448]{1,0:T(8,128)} %param.22, f32[48,6448]{1,0:T(8,128)} %param.23), kind=kLoop, calls=%fused_computation.26 | loop fusion | flops 5261568 | bytes 8666112 | tf_op jit(solution)/shard_map/sub | solution.py:176
  402.4 1.5 convert_reduce_fusion.1
  403.9 0.6 dynamic-slice.17
  404.6 0.6 compare_convert_fusion
  405.3 4.9 %fusion.2 = (f32[256,1536]{1,0:T(8,128)}, bf16[256,1536]{1,0:T(8,128)(2,1)}) fusion(bf16[256,1536]{1,0:T(8,128)(2,1)} %tok.1, bf16[256,1536]{1,0:T(8,128)(2,1)} %cot.1, f32[256]{0:T(256)S(1)} %multiply_multiply_fusion.5, f32[256]{0:T(256)S(1)} %fusion.23, f32[1536]{0:T(1024)S(1)} %slice.113, f32[256,1536]{1,0:T(8,128)} %copy-done.1, ...), kind=kLoop, calls=%fused_computation.15 | loop fusion | flops 5898240 | bytes 8659972 | tf_op jit(solution)/shard_map/add | solution.py:1450
  410.3 0.9 copy-done.6
  411.5 1.5 multiply_subtract_fusion.1
  (128 shorter events, 5.1 us)
Async XLA Ops:
  3.1 1.9 copy-start.14
  3.1 2.2 copy-start.20
  3.2 2.3 copy-start.23
  3.7 2.7 copy-start.5
  113.7 4.2 %copy-start.15 = (f32[3,48]{1,0:T(4,128)S(1)}, f32[3,48]{1,0:T(4,128)}, u32[]{:S(2)}) copy-start(f32[3,48]{1,0:T(4,128)} %param.33) | copy-start | bytes 1732
  231.7 6.0 %slice-start = ((s8[6291456]{0:T(1024)(128)(4,1)}), s8[4194304]{0:T(1024)(128)(4,1)S(1)}, s32[]{:S(2)}) async-start(s8[6291456]{0:T(1024)(128)(4,1)} %bitcast.91), calls=%async_computation | async-start | bytes 8388608
  231.7 6.0 %slice-start.1 = ((s8[6291456]{0:T(1024)(128)(4,1)}), s8[2097152]{0:T(1024)(128)(4,1)S(1)}, s32[]{:S(2)}) async-start(s8[6291456]{0:T(1024)(128)(4,1)} %bitcast.91), calls=%async_computation.1 | async-start | bytes 4194304
  237.7 3.4 copy-start.8
  242.2 11.4 %copy-start.3 = (bf16[16,2,48,384]{3,2,0,1:T(8,128)(2,1)S(1)}, bf16[16,2,48,384]{3,2,0,1:T(8,128)(2,1)}, u32[]{:S(2)}) copy-start(bf16[16,2,48,384]{3,2,0,1:T(8,128)(2,1)} %copy.89) | copy-start | bytes 3538948
  343.5 2.4 copy-start.2
  343.5 2.8 copy-start
  345.9 1.1 copy-start.1
  346.3 1.1 copy-start.13
  347.0 13.2 %copy-start.16 = (f32[5,104]{1,0:T(8,128)S(1)}, f32[5,104]{1,0:T(8,128)}, u32[]{:S(2)}) copy-start(f32[5,104]{1,0:T(8,128)} %param.28) | copy-start | bytes 6244
  347.0 13.2 %copy-start.17 = (f32[5,104]{1,0:T(8,128)S(1)}, f32[5,104]{1,0:T(8,128)}, u32[]{:S(2)}) copy-start(f32[5,104]{1,0:T(8,128)} %param.29) | copy-start | bytes 6244
  347.0 13.8 %copy-start.21 = (f32[144]{0:T(256)S(1)}, f32[144]{0:T(256)}, u32[]{:S(2)}) copy-start(f32[144]{0:T(256)} %param.31) | copy-start | bytes 1732
  347.0 13.8 %copy-start.22 = (f32[144]{0:T(256)S(1)}, f32[144]{0:T(256)}, u32[]{:S(2)}) copy-start(f32[144]{0:T(256)} %param.32) | copy-start | bytes 1732
  347.1 14.5 %copy-start.18 = (f32[3,48]{1,0:T(4,128)S(1)}, f32[3,48]{1,0:T(4,128)}, u32[]{:S(2)}) copy-start(f32[3,48]{1,0:T(4,128)} %param.34) | copy-start | bytes 1732
  347.1 14.5 %copy-start.19 = (f32[3,48]{1,0:T(4,128)S(1)}, f32[3,48]{1,0:T(4,128)}, u32[]{:S(2)}) copy-start(f32[3,48]{1,0:T(4,128)} %param.35) | copy-start | bytes 1732
  364.0 2.1 copy-start.11
  391.3 5.2 %copy-start.12 = (bf16[3,48,384]{2,1,0:T(8,128)(2,1)S(1)}, bf16[3,48,384]{2,1,0:T(8,128)(2,1)}, u32[]{:S(2)}) copy-start(bf16[3,48,384]{2,1,0:T(8,128)(2,1)} %get-tuple-element.74) | copy-start | bytes 331780
  397.4 5.0 %copy-start.4 = (bf16[3,256,1536]{2,1,0:T(8,128)(2,1)S(1)}, bf16[3,256,1536]{2,1,0:T(8,128)(2,1)}, u32[]{:S(2)}) copy-start(bf16[3,256,1536]{2,1,0:T(8,128)(2,1)} %get-tuple-element.69) | copy-start | bytes 7077892
  405.3 4.9 %copy-start.7 = (bf16[4,96,1536]{2,1,0:T(8,128)(2,1)S(1)}, bf16[4,96,1536]{2,1,0:T(8,128)(2,1)}, u32[]{:S(2)}) copy-start(bf16[4,96,1536]{2,1,0:T(8,128)(2,1)} %get-tuple-element.75) | copy-start | bytes 3538948
  410.1 1.1 copy-start.6
  410.1 1.2 copy-start.9
  410.1 1.4 copy-start.10
